TPU v7x, 512 devices: a whole 4x8x8 slice. The times are simulated.
512 devices in a mesh: dp: 16 (over z, core), ent: 32 (over y, x).
Axes of the slice: x: 4, y: 8, z: 8, core: 2. Of those that a mesh axis runs over, the one named last changes fastest.
Arguments:
- entity_table: float32 [16384, 1024], P('ent')
- adagrad_state: float32 [16384], P('ent'), may hold values from 0.0001 to 0.01
- relation_phase: float32 [448, 512], replicated, may hold values from -3.140625 to 3.140625
- head_owner: int32 [65536, 1], P(('dp', 'ent')), may hold values from 0 to 31; in each aligned block of 128 rows (0 to 127, 128 to 255, ...) at most 12 rows name the same one
- head_row: int32 [65536], P(('dp', 'ent')), may hold values from 0 to 511
- relation_id: int32 [65536], P(('dp', 'ent')), may hold values from 0 to 447
- tail_row: int32 [65536], P(('dp', 'ent')), may hold values from 0 to 511
- negative_row: int32 [1048576], P(('dp', 'ent')), may hold values from 0 to 511
Outputs:
- new_table: float32 [16384, 1024], P('ent')
- new_state: float32 [16384], P('ent')
Inputs may be any that keep to these rules, and one draw needn't show every extreme that they name: `head_owner`: within each aligned block of 128 triples (those of one device) no index is named more than 12 times, a bound that some block reaches.
All inputs are finite; a program needn't handle non-finite values.
Results may differ from a plain program's by a relative error of at most 0.0014.
Values may be sent and summed in bfloat16 or wider, within the bound.
A program may use at most 64 MiB of HBM per device.

v0:
```python
import jax
import jax.numpy as jnp
from jax import lax
from jax.sharding import PartitionSpec as P

MARGIN = 12.0
LEARN_RATE = 0.25


def rotate(real_part, imag_part, cosine, sine_val):
    return (real_part * cosine - imag_part * sine_val, real_part * sine_val + imag_part * cosine)


def adagrad(rows_in, acc_in, gradient):
    new_acc = acc_in + jnp.mean(gradient * gradient, axis=1)
    return (rows_in - LEARN_RATE * gradient / jnp.sqrt(new_acc)[:, None], new_acc)


def on_device(
    entity_table,
    adagrad_state,
    relation_phase,
    head_owner,
    head_row,
    relation_id,
    tail_row,
    negative_row,
):
    owners = lax.axis_size("ent")
    tri_rows = head_row.shape[0]
    local_rows = entity_table.shape[0]
    half = entity_table.shape[1] // 2
    capacity = 3 * tri_rows // owners
    owner_ids = head_owner[:, 0]
    onehot = (owner_ids[:, None] == jnp.arange(owners, dtype=jnp.int32)[None, :]).astype(jnp.int32)
    rank_in = jnp.sum((jnp.cumsum(onehot, axis=0) - 1) * onehot, axis=1)
    slot_ids = owner_ids * capacity + rank_in
    requests = (
        jnp.zeros((owners * capacity,), jnp.int32)
        .at[slot_ids]
        .set(head_row)
        .reshape(owners, capacity)
    )
    table_bf = entity_table.astype(jnp.bfloat16)
    asked_ids = lax.all_to_all(requests, "ent", split_axis=0, concat_axis=0, tiled=True)
    fetched = jnp.take(table_bf, asked_ids, axis=0)
    replies = lax.all_to_all(fetched, "ent", split_axis=0, concat_axis=0, tiled=True)
    head_rows = jnp.take(replies.reshape(owners * capacity, 2 * half), slot_ids, axis=0).astype(
        jnp.float32
    )
    angles = jnp.take(relation_phase, relation_id, axis=0)
    cosine = jnp.cos(angles)
    sine_val = jnp.sin(angles)
    rot_re, rot_im = rotate(head_rows[:, :half], head_rows[:, half:], cosine, sine_val)
    rotated = jnp.concatenate([rot_re, rot_im], axis=1)
    rotated_bf = rotated.astype(jnp.bfloat16)
    negative_bf = jnp.take(table_bf, negative_row, axis=0)
    neg_scores = jnp.dot(rotated_bf, negative_bf.T, preferred_element_type=jnp.float32)
    selector = (negative_row[:, None] == jnp.arange(local_rows, dtype=jnp.int32)[None, :]).astype(
        jnp.float32
    )
    rot_sq = jnp.sum(rotated * rotated, axis=1)
    row_sq = jnp.sum(entity_table * entity_table, axis=1)
    neg_sq = jnp.dot(selector, row_sq, precision=lax.Precision.HIGHEST)
    distance = (rot_sq[:, None] + neg_sq[None, :] - 2.0 * neg_scores) / half
    positive = jnp.take(entity_table, tail_row, axis=0)
    diff_pos = rotated - positive
    dist_pos = jnp.sum(diff_pos * diff_pos, axis=1) / half
    logits = MARGIN - distance
    shifted = jnp.exp(logits - jnp.max(logits, axis=1, keepdims=True))
    weights = shifted / jnp.sum(shifted, axis=1, keepdims=True)
    neg_coef = -0.5 * weights * jax.nn.sigmoid(MARGIN - distance)
    pos_coef = 0.5 * jax.nn.sigmoid(dist_pos - MARGIN)
    row_coef = jnp.dot(neg_coef, selector, precision=lax.Precision.HIGHEST)
    row_coef_bf = row_coef.astype(jnp.bfloat16)
    total_coef = pos_coef + jnp.sum(row_coef, axis=1)
    pulled = jnp.dot(row_coef_bf, table_bf, preferred_element_type=jnp.float32)
    grad_query = (
        2.0 / half * (total_coef[:, None] * rotated - pos_coef[:, None] * positive - pulled)
    )
    grad_re, grad_im = rotate(grad_query[:, :half], grad_query[:, half:], cosine, -sine_val)
    grad_head = jnp.concatenate([grad_re, grad_im], axis=1)
    outgoing = (
        jnp.zeros((owners * capacity, 2 * half), jnp.float32)
        .at[slot_ids]
        .set(grad_head)
        .reshape(owners, capacity, 2 * half)
    )
    incoming = lax.all_to_all(
        outgoing.astype(jnp.bfloat16), "ent", split_axis=0, concat_axis=0, tiled=True
    ).astype(outgoing.dtype)
    head_part = jax.ops.segment_sum(
        incoming.reshape(owners * capacity, 2 * half),
        asked_ids.reshape(owners * capacity),
        num_segments=local_rows,
    )
    tail_pull = jnp.dot(row_coef_bf.T, rotated_bf, preferred_element_type=jnp.float32)
    column_coef = jnp.sum(row_coef, axis=0)
    tail_part = 2.0 / half * (column_coef[:, None] * entity_table - tail_pull)
    tail_part = tail_part + jax.ops.segment_sum(
        -2.0 / half * pos_coef[:, None] * diff_pos, tail_row, num_segments=local_rows
    )
    local_grad = head_part + tail_part
    summed = lax.psum(local_grad.astype(jnp.bfloat16), "dp").astype(jnp.float32)
    new_table, new_state = adagrad(entity_table, adagrad_state, summed)
    return (new_table, new_state)


def solution(mesh):
    return jax.shard_map(
        on_device,
        mesh=mesh,
        in_specs=(
            P("ent", None),
            P("ent"),
            P(),
            P(("dp", "ent"), None),
            P(("dp", "ent")),
            P(("dp", "ent")),
            P(("dp", "ent")),
            P(("dp", "ent")),
        ),
        out_specs=(P("ent", None), P("ent")),
        check_vma=False,
    )
```

profile of v0, /device:TPU:1, one launch (start us, length us, event | category | flops | bytes accessed | tf_op | source)
XLA Modules:
  0.0 267.5 jit_solution(844240439098383927)
XLA Ops:
  7.2 0.0 copy-start
  7.2 0.8 fusion.49
  8.0 0.2 reduce_window_sum.11
  8.2 0.8 select_reduce_fusion
  9.0 1.2 and_bitcast_fusion
  10.2 1.1 scatter_custom_fusion
  11.3 0.7 all_to_all.16
  12.0 10.5 %all-to-all-start = ((s32[32,1,12]{2,1,0:T(1,128)}), s32[32,1,12]{2,1,0:T(1,128)S(1)}, u32[]{:S(2)}, u32[]{:S(2)}) async-start(s32[32,1,12]{2,1,0:T(1,128)} %bitcast.3), calls=%async_computation | async-start | bytes 32768 | tf_op jit(solution)/shard_map/all_to_all | solution.py:45
  22.5 0.7 compare_select_fusion.3
  23.2 3.1 %multiply_reduce_fusion = (f32[512]{0:T(512)}, bf16[512,1024]{1,0:T(8,128)(2,1)S(1)}) fusion(f32[512,1024]{1,0:T(8,128)} %param.8), kind=kLoop, calls=%fused_computation.27 | loop fusion | flops 1572352 | bytes 3147776 | tf_op jit(solution)/shard_map/reduce_sum | solution.py:63
  26.3 2.6 gather_fusion.3
  28.9 2.1 all-to-all-done
  31.1 0.1 reshape.107
  31.2 2.1 gather_fusion
  33.3 1.1 reshape.106
  34.4 2.4 broadcast_select_fusion
  36.8 7.3 %all-to-all-start.1 = ((bf16[32,12,1024]{2,1,0:T(8,128)(2,1)}), bf16[32,12,1024]{2,1,0:T(8,128)(2,1)}, u32[]{:S(2)}, u32[]{:S(2)}) async-start(bf16[32,12,1024]{2,1,0:T(8,128)(2,1)} %broadcast_select_fusion), calls=%async_computation.1 | async-start | bytes 2097152 | tf_op jit(solution)/shard_map/all_to_all | solution.py:47
  44.1 0.0 copy-start.16
  44.1 9.7 %gather_fusion.4 = bf16[2048,1024]{1,0:T(8,128)(2,1)} fusion(bf16[512,1024]{1,0:T(8,128)(2,1)S(1)} %get-tuple-element.13, s32[2048]{0:T(1024)S(1)} %fusion.52), kind=kCustom, calls=%fused_computation.4 | custom fusion | bytes 8396800 | tf_op jit(solution)/shard_map/jit(_take)/gather | solution.py:57
  53.8 0.0 copy-start.14
  53.8 0.8 gather_fusion.2
  54.6 0.6 pad_clamp_fusion.2
  55.2 0.0 copy-done.17
  55.2 0.5 compare_and_fusion.2
  55.7 0.5 compare_and_fusion.3
  56.2 0.6 compare_and_fusion.1
  56.8 2.8 %fusion.3 = f32[1,2048]{1,0:T(1,128)} fusion(f32[512,1]{0,1:T(1,128)S(1)} %bitcast.29, s32[2048]{0:T(1024)S(1)} %copy-done.5), kind=kOutput, calls=%fused_computation.13 | convolution fusion | flops 13631488 | bytes 18432 | tf_op jit(solution)/shard_map/dot_general | solution.py:64
  59.6 10.1 %all-to-all-done.1 = bf16[32,12,1024]{2,1,0:T(8,128)(2,1)} async-done(((bf16[32,12,1024]{2,1,0:T(8,128)(2,1)}), bf16[32,12,1024]{2,1,0:T(8,128)(2,1)}, u32[]{:S(2)}, u32[]{:S(2)}) %all-to-all-start.1) | async-done | bytes 786464 | tf_op jit(solution)/shard_map/all_to_all | solution.py:47
  69.7 1.3 reshape.100
  71.0 1.7 gather_fusion.1
  72.7 1.1 select_convert_fusion
  73.8 1.8 multiply_subtract_fusion.1
  75.6 0.0 copy-start.2
  75.6 0.0 copy-start.3
  75.6 0.0 copy-done.7
  75.6 0.2 multiply_reduce_fusion.1
  75.8 0.6 broadcast_multiply_fusion
  76.4 0.0 copy-done.10
  76.4 3.6 %fusion.63 = (f32[128]{0:T(128)S(1)}, f32[128,2048]{1,0:T(8,128)S(1)}) fusion(bf16[2048,1024]{1,0:T(8,128)(2,1)} %gather_fusion.4, pred[2048]{0:T(1024)(128)(4,1)S(1)} %copy-done.10, f32[128,512]{1,0:T(8,128)S(1)} %get-tuple-element.17, f32[128,512]{1,0:T(8,128)S(1)} %get-tuple-element.16, f32[2048]{0:T(1024)S(1)} %bitcast.30, f32[128]{0:T(128)S(1)} %get-tuple-element.2), kind=kOutput, calls=%fused_computation.104 | convolution fusion | flops 541065088 | bytes 5778432 | tf_op jit(solution)/shard_map/dot_general | solution.py:58
  80.1 0.3 fusion.31
  80.4 2.6 fusion.61
  83.0 0.0 copy-done.2
  83.0 0.6 copy-done.4
  83.6 0.3 fusion.23
  83.9 1.8 multiply_subtract_fusion
  85.8 1.8 scatter_custom_fusion.1
  87.6 1.0 convert_element_type.34
  88.6 2.3 convert_element_type.35
  90.9 6.8 %all-to-all-start.2 = ((bf16[32,12,1024]{2,1,0:T(8,128)(2,1)}), bf16[32,12,1024]{2,1,0:T(8,128)(2,1)}, u32[]{:S(2)}, u32[]{:S(2)}) async-start(bf16[32,12,1024]{2,1,0:T(8,128)(2,1)} %convert_element_type.35), calls=%async_computation.2 | async-start | bytes 2097152 | tf_op jit(solution)/shard_map/all_to_all | solution.py:89
  97.7 0.0 all-reduce.2.cloned.1.call-start
  97.7 0.5 broadcast.191
  98.2 1.3 reduce.3
  99.5 0.8 reshape.163
  100.4 2.9 %subtract_multiply_fusion = f32[512,1024]{1,0:T(8,128)} fusion(f32[512,1024]{1,0:T(8,128)S(1)} %copy-done.1, f32[512]{0:T(512)} %get-tuple-element.4, bf16[128,512]{1,0:T(8,128)(2,1)} %copy-done.4, f32[128,512]{1,0:T(8,128)} %copy-done.3, f32[128,512]{1,0:T(8,128)} %copy-done.2), kind=kOutput, calls=%fused_computation.25 | convolution fusion | flops 136314880 | bytes 4851712 | tf_op jit(solution)/shard_map/dot_general | solution.py:97
  103.3 5.1 %scatter_custom_fusion.3 = f32[512,1024]{1,0:T(8,128)} fusion(f32[512,1024]{1,0:T(8,128)} %subtract_multiply_fusion, s32[128]{0:T(128)} %param.14, f32[128]{0:T(128)S(1)} %copy-done.15, f32[128,1024]{1,0:T(8,128)S(1)} %gather_fusion.3, pred[128]{0:T(512)(128)(4,1)S(1)} %copy-done.8, f32[128,512]{1,0:T(8,128)} %copy-done.3, f32[128,512]{1,0:T(8,128)} %copy-done.2), kind=kCustom, calls=%fused_computation.50 | custom fusion | flops 655360 | bytes 3146368 | tf_op jit(solution)/shard_map/scatter-add | solution.py:100
  108.4 13.9 %all-to-all-done.2 = bf16[32,12,1024]{2,1,0:T(8,128)(2,1)} async-done(((bf16[32,12,1024]{2,1,0:T(8,128)(2,1)}), bf16[32,12,1024]{2,1,0:T(8,128)(2,1)}, u32[]{:S(2)}, u32[]{:S(2)}) %all-to-all-start.2) | async-done | bytes 786464 | tf_op jit(solution)/shard_map/all_to_all | solution.py:89
  122.3 2.3 reshape.165
  124.6 5.9 %scatter_custom_fusion.2 = f32[512,1024]{1,0:T(8,128)} fusion(s32[384]{0:T(512)S(1)} %reshape.163, f32[384,1024]{1,0:T(8,128)} %reshape.165, f32[]{:T(128)} %constant.52.clone.1), kind=kCustom, calls=%fused_computation.41 | custom fusion | flops 393216 | bytes 2097664 | tf_op jit(solution)/shard_map/scatter-add | solution.py:92
  130.5 3.5 %add_convert_fusion = bf16[512,1024]{1,0:T(8,128)(2,1)} fusion(f32[512,1024]{1,0:T(8,128)} %scatter_custom_fusion.2, f32[512,1024]{1,0:T(8,128)} %scatter_custom_fusion.3), kind=kLoop, calls=%fused_computation.24 | loop fusion | flops 1048576 | bytes 5242880 | tf_op jit(solution)/shard_map/convert_element_type | solution.py:104
  134.1 0.0 all-reduce.2.cloned.1.call-update
  134.1 121.6 %all-reduce.2.cloned.1.call-done = bf16[512,1024]{1,0:T(8,128)(2,1)} async-done(((bf16[512,1024]{1,0:T(8,128)(2,1)}), bf16[512,1024]{1,0:T(8,128)(2,1)}) %all-reduce.2.cloned.1.call-update) | async-done | bytes 1048592 | tf_op jit(solution)/shard_map/psum | solution.py:104
  255.7 1.5 fusion.19
  257.2 0.6 fusion.62
  257.7 2.9 %fusion.18 = f32[512,1024]{1,0:T(8,128)} fusion(f32[512,1024]{1,0:T(8,128)S(1)} %copy-done.1, bf16[512,1024]{1,0:T(8,128)(2,1)} %all-reduce.2.cloned.1.call-done, f32[512]{0:T(512)S(1)} %get-tuple-element.6), kind=kLoop, calls=%fused_computation.22 | loop fusion | flops 2097152 | bytes 5244928 | tf_op jit(solution)/shard_map/sub | solution.py:16
  (36 shorter events, 0.1 us)
Async XLA Ops:
  7.2 46.6 %copy-start = (f32[448,512]{1,0:T(8,128)S(1)}, f32[448,512]{1,0:T(8,128)}, u32[]{:S(2)}) copy-start(f32[448,512]{1,0:T(8,128)} %param.10) | copy-start | bytes 2752516
  10.2 16.1 %copy-start.11 = (s32[128,1]{0,1:T(1,128)}, s32[128,1]{0,1:T(1,128)S(1)}, u32[]{:S(2)}) copy-start(s32[128,1]{0,1:T(1,128)S(1)} %get-tuple-element.11) | copy-start | bytes 1540
  12.0 19.0 %all-to-all-start = ((s32[32,1,12]{2,1,0:T(1,128)}), s32[32,1,12]{2,1,0:T(1,128)S(1)}, u32[]{:S(2)}, u32[]{:S(2)}) async-start(s32[32,1,12]{2,1,0:T(1,128)} %bitcast.3), calls=%async_computation | async-start | bytes 32768 | tf_op jit(solution)/shard_map/all_to_all | solution.py:45
  34.4 9.6 %copy-start.5 = (s32[2048]{0:T(1024)S(1)}, s32[2048]{0:T(1024)}, u32[]{:S(2)}) copy-start(s32[2048]{0:T(1024)} %param.15) | copy-start | bytes 24580
  36.8 32.9 %all-to-all-start.1 = ((bf16[32,12,1024]{2,1,0:T(8,128)(2,1)}), bf16[32,12,1024]{2,1,0:T(8,128)(2,1)}, u32[]{:S(2)}, u32[]{:S(2)}) async-start(bf16[32,12,1024]{2,1,0:T(8,128)(2,1)} %broadcast_select_fusion), calls=%async_computation.1 | async-start | bytes 2097152 | tf_op jit(solution)/shard_map/all_to_all | solution.py:47
  44.1 9.7 %copy-start.16 = (s32[128]{0:T(128)S(1)}, s32[128]{0:T(128)}, u32[]{:S(2)}) copy-start(s32[128]{0:T(128)} %param.13) | copy-start | bytes 1540
  53.7 0.8 copy-start.12
  53.7 1.4 copy-start.17
  53.8 3.1 %copy-start.14 = (f32[512]{0:T(512)S(1)}, f32[512]{0:T(512)}, u32[]{:S(2)}) copy-start(f32[512]{0:T(512)} %get-tuple-element.12) | copy-start | bytes 6148
  72.7 2.9 %copy-start.7 = (pred[128]{0:T(512)(128)(4,1)S(1)}, pred[128]{0:T(512)(128)(4,1)}, u32[]{:S(2)}) copy-start(pred[128]{0:T(512)(128)(4,1)} %compare_and_fusion.2) | copy-start | bytes 388
  72.7 3.7 %copy-start.10 = (pred[2048]{0:T(1024)(128)(4,1)S(1)}, pred[2048]{0:T(1024)(128)(4,1)}, u32[]{:S(2)}) copy-start(pred[2048]{0:T(1024)(128)(4,1)} %compare_and_fusion.1) | copy-start | bytes 6148
  72.7 3.7 %copy-start.18 = (f32[1,2048]{1,0:T(1,128)S(1)}, f32[1,2048]{1,0:T(1,128)}, u32[]{:S(2)}) copy-start(f32[1,2048]{1,0:T(1,128)} %fusion.3) | copy-start | bytes 24580
  75.6 7.4 %copy-start.2 = (f32[128,512]{1,0:T(8,128)}, f32[128,512]{1,0:T(8,128)S(1)}, u32[]{:S(2)}) copy-start(f32[128,512]{1,0:T(8,128)S(1)} %get-tuple-element.16) | copy-start | bytes 786436
  75.6 7.4 %copy-start.3 = (f32[128,512]{1,0:T(8,128)}, f32[128,512]{1,0:T(8,128)S(1)}, u32[]{:S(2)}) copy-start(f32[128,512]{1,0:T(8,128)S(1)} %get-tuple-element.17) | copy-start | bytes 786436
  76.4 4.0 %copy-start.6 = (s32[2048]{0:T(1024)S(1)}, s32[2048]{0:T(1024)}, u32[]{:S(2)}) copy-start(s32[2048]{0:T(1024)} %param.15) | copy-start | bytes 24580
  82.9 0.7 copy-start.4
  82.9 1.0 copy-start.9
  88.6 11.7 %copy-start.1 = (f32[512,1024]{1,0:T(8,128)S(1)}, f32[512,1024]{1,0:T(8,128)}, u32[]{:S(2)}) copy-start(f32[512,1024]{1,0:T(8,128)} %param.8) | copy-start | bytes 6291460
  90.9 31.4 %all-to-all-start.2 = ((bf16[32,12,1024]{2,1,0:T(8,128)(2,1)}), bf16[32,12,1024]{2,1,0:T(8,128)(2,1)}, u32[]{:S(2)}, u32[]{:S(2)}) async-start(bf16[32,12,1024]{2,1,0:T(8,128)(2,1)} %convert_element_type.35), calls=%async_computation.2 | async-start | bytes 2097152 | tf_op jit(solution)/shard_map/all_to_all | solution.py:89
  97.7 158.0 %all-reduce.2.cloned.1.call-start = ((), (), s32[]{:S(2)}) async-start(), calls=%async_computation.3 | async-start | bytes 2097152 | tf_op jit(solution)/shard_map/psum | solution.py:104
  100.3 2.9 %copy-start.8 = (pred[128]{0:T(512)(128)(4,1)S(1)}, pred[128]{0:T(512)(128)(4,1)}, u32[]{:S(2)}) copy-start(pred[128]{0:T(512)(128)(4,1)} %compare_and_fusion.2) | copy-start | bytes 388
  100.3 2.9 %copy-start.15 = (f32[128]{0:T(128)S(1)}, f32[128]{0:T(128)}, u32[]{:S(2)}) copy-start(f32[128]{0:T(128)} %get-tuple-element.8) | copy-start | bytes 1540
  134.1 123.1 %copy-start.13 = (f32[512]{0:T(512)S(1)}, f32[512]{0:T(512)}, u32[]{:S(2)}) copy-start(f32[512]{0:T(512)} %param.9) | copy-start | bytes 6148
Sparse Core Ops, SparseCore 0:
  134.2 121.3 all-reduce.1
where the time goes:
time: 268 us
  waiting for transfers between devices  148 us (55%)
  other arithmetic  40.9 us (15%)
  local copies, waits for them, and re-layouts  27.9 us (10%)
  starting transfers between devices  24.6 us (9%)
  between operations  14.3 us (5%)
  matrix products  12.2 us (5%)
    psum x1, waiting for transfers between devices, on_device(): summed = lax.psum(local_grad.astype(jnp.bfloat16), 'dp').astype(jnp.float32)  122 us
    all_to_all x1, waiting for transfers between devices, on_device(): lax.all_to_all(outgoing.astype(jnp.bfloat16), 'ent', split_axis=0, concat...  13.9 us
    all_to_all x1, starting transfers between devices, on_device(): lax.all_to_all(requests, 'ent', split_axis=0, concat_axis=0, tiled=True)  10.5 us
    all_to_all x1, waiting for transfers between devices, on_device(): lax.all_to_all(fetched, 'ent', split_axis=0, concat_axis=0, tiled=True)  10.1 us
    gather x1, local copies, waits for them, and re-layouts, on_device(): negative_bf = jnp.take(table_bf, negative_row, axis=0)  9.67 us
    all_to_all x1, starting transfers between devices, on_device(): lax.all_to_all(fetched, 'ent', split_axis=0, concat_axis=0, tiled=True)  7.26 us
    all_to_all x1, starting transfers between devices, on_device(): lax.all_to_all(outgoing.astype(jnp.bfloat16), 'ent', split_axis=0, concat...  6.77 us
    scatter-add x1, other arithmetic, on_device(): jax.ops.segment_sum(incoming.reshape(owners * capacity, 2 * half), asked_...  5.9 us
  transfers between devices with their start and end apart: 4, of which 4 were waited for; matrix products, arithmetic and copies ran while one was open for 12% of the time, Pallas kernels for 0%

commit v1 on v0

v1 whole, which is shorter than its diff:
```python
import functools

import jax
import jax.numpy as jnp
from jax import lax
from jax.experimental import pallas as pl
from jax.experimental.pallas import tpu as pltpu
from jax.sharding import PartitionSpec as P

MARGIN = 12.0
LEARN_RATE = 0.25
F32 = jnp.float32
BF16 = jnp.bfloat16
LANES = 128


def onehot(condition):
    return jnp.where(condition, 1.0, 0.0).astype(BF16)


def iota(shape, dim):
    return lax.broadcasted_iota(jnp.int32, shape, dim)


def to_column(row):
    wide = jnp.broadcast_to(row, (LANES, row.shape[1]))
    return jnp.transpose(wide)[:, 0:1]


def to_row(column):
    wide = jnp.broadcast_to(column, (column.shape[0], LANES))
    return jnp.transpose(wide)[0:1, :]


def dot(a, b):
    return jnp.dot(a, b, preferred_element_type=F32)


def dot_nt(a, b, precision=None):
    return lax.dot_general(
        a, b, (((1,), (1,)), ((), ())), preferred_element_type=F32, precision=precision
    )


def split3(x):
    first = x.astype(BF16)
    rest = x - first.astype(F32)
    second = rest.astype(BF16)
    third = (rest - second.astype(F32)).astype(BF16)
    return first, second, third


def kernel(
    n_ent,
    n_dp,
    cap,
    table_hbm,
    state_ref,
    phase_hbm,
    owner_ref,
    hrow_ref,
    rel_ref,
    tail_ref,
    neg_ref,
    out_table,
    out_state,
    table,
    table_bf,
    phase,
    flat,
    req_send,
    req_recv,
    rep_send,
    rep_recv,
    gr_send,
    gr_recv,
    pick,
    pick_t,
    asked,
    asked_t,
    tail_hot,
    row_sq,
    count,
    positive,
    cosine,
    sine,
    rotated,
    partial,
    pair_send,
    pair_recv,
    z_send,
    z_recv,
    total,
    state_col,
    sems,
):
    rows, width = table.shape
    half = width // 2
    tri = hrow_ref.shape[1]
    negs = neg_ref.shape[1]
    rels = phase.shape[0]
    slots = n_ent * cap
    chunks = width // LANES
    blk = cap * chunks
    nz = n_dp // 2
    hrows = rows // 2
    prow = rows // n_dp
    ny = n_ent // 4 if n_ent > 4 else 2
    nx = n_ent // ny
    tile = 256
    tiles = width // tile

    ent = lax.axis_index("ent")
    dp = lax.axis_index("dp")
    z = lax.div(dp, 2)
    core = lax.rem(dp, 2)
    y = lax.div(ent, nx)
    x = lax.rem(ent, nx)
    partner = dp + 1 - 2 * core

    def turn(m, n):
        odd = lax.rem(m, 2)
        return lax.rem((2 * odd - 1) * lax.div(m + 1, 2) + n, n)

    def ent_peer(k):
        dy = turn(lax.rem(k, ny), ny)
        dx = lax.div(k, ny)
        return lax.rem(y + dy, ny) * nx + lax.rem(x + dx, nx)

    def z_peer(k):
        return lax.rem(z + turn(nz - k, nz), nz)

    def remote(src, dst, first_sem, axis, index):
        return pltpu.make_async_remote_copy(
            src_ref=src,
            dst_ref=dst,
            send_sem=sems.at[first_sem],
            recv_sem=sems.at[first_sem + 1],
            device_id={axis: index},
            device_id_type=pl.DeviceIdType.MESH,
        )

    load_table = pltpu.make_async_copy(table_hbm, table, sems.at[0])
    load_phase = pltpu.make_async_copy(phase_hbm, phase, sems.at[1])
    load_table.start()
    load_phase.start()

    barrier = pltpu.get_barrier_semaphore()

    def greet_ent(k, carry):
        pl.semaphore_signal(
            barrier, inc=1, device_id={"ent": ent_peer(k)}, device_id_type=pl.DeviceIdType.MESH
        )
        return carry

    def greet_z(k, carry):
        pl.semaphore_signal(
            barrier,
            inc=1,
            device_id={"dp": 2 * z_peer(k) + core},
            device_id_type=pl.DeviceIdType.MESH,
        )
        return carry

    lax.fori_loop(1, n_ent, greet_ent, 0)
    lax.fori_loop(1, nz, greet_z, 0)
    pl.semaphore_signal(
        barrier, inc=1, device_id={"dp": partner}, device_id_type=pl.DeviceIdType.MESH
    )

    owner_row = owner_ref[...]
    own_hot = owner_row == iota((n_ent, tri), 0)
    own_bf = onehot(own_hot)
    before = onehot(iota((tri, tri), 0) < iota((tri, tri), 1))
    prior = dot(own_bf, before)
    rank = jnp.sum(jnp.where(own_hot, prior, 0.0), axis=0, keepdims=True).astype(jnp.int32)
    slot_row = owner_row * cap + rank
    lane_row = lax.rem(ent * cap + rank, LANES)
    lane_hot = onehot(lane_row == iota((LANES, tri), 0))
    wanted = hrow_ref[...] + 1
    high = lax.shift_right_logical(wanted, 5)
    low = wanted - high * 32
    high_part = jnp.where(own_hot, high.astype(F32), 0.0).astype(BF16)
    low_part = jnp.where(own_hot, low.astype(F32), 0.0).astype(BF16)
    request = dot_nt(high_part, lane_hot) * 32.0 + dot_nt(low_part, lane_hot)
    for o in range(n_ent):
        req_send[o] = request[o : o + 1, :]

    pl.semaphore_wait(barrier, n_ent - 1 + nz - 1 + 1)

    def send_request(k, carry):
        q = ent_peer(k)
        remote(req_send.at[q], req_recv.at[ent], 2, "ent", q).start()
        return carry

    lax.fori_loop(1, n_ent, send_request, 0)
    req_recv[ent] = req_send[ent]

    load_table.wait()

    def cast_table(j, carry):
        columns = pl.ds(pl.multiple_of(j * tile, tile), tile)
        table_bf[:, columns] = table[:, columns].astype(BF16)
        return carry

    lax.fori_loop(0, tiles, cast_table, 0)

    got = remote(
        req_send.at[pl.ds(0, n_ent - 1)], req_recv.at[pl.ds(0, n_ent - 1)], 2, "ent", ent_peer(1)
    )
    got.wait_recv()
    got.wait_send()

    inbox = jnp.concatenate([req_recv[o] for o in range(n_ent)], axis=0)
    first = iota((n_ent, LANES), 0) * cap
    lane = iota((n_ent, LANES), 1)
    offset = lax.rem(lane - first + LANES * n_ent, LANES)
    vreg = lax.shift_right_logical(first + offset, 7)
    ask_parts = []
    for v in range(-(-slots // LANES)):
        mine = jnp.logical_and(offset < cap, vreg == v)
        ask_parts.append(jnp.sum(jnp.where(mine, inbox, 0.0), axis=0, keepdims=True))
    ask_row = jnp.concatenate(ask_parts, axis=1)[:, :slots].astype(jnp.int32) - 1
    ask_col = to_column(ask_row)
    asked_t[...] = onehot(ask_col == iota((slots, rows), 1))

    def fetch(j, carry):
        columns = pl.ds(pl.multiple_of(j * tile, tile), tile)
        part = dot(asked_t[...], table_bf[:, columns])
        flat[pl.ds(2 * j, slots, stride=chunks), :] = part[:, :LANES]
        flat[pl.ds(2 * j + 1, slots, stride=chunks), :] = part[:, LANES:]
        return carry

    lax.fori_loop(0, tiles, fetch, 0)

    def send_rows(source, target, first_sem):
        def body(k, carry):
            q = ent_peer(k)
            block = pl.ds(pl.multiple_of(q * blk, 16), blk)
            source[block, :] = flat[block, :].astype(BF16)
            remote(
                source.at[block],
                target.at[pl.ds(pl.multiple_of(ent * blk, 16), blk)],
                first_sem,
                "ent",
                q,
            ).start()
            return carry

        lax.fori_loop(1, n_ent, body, 0)
        own = pl.ds(pl.multiple_of(ent * blk, 16), blk)
        target[own, :] = flat[own, :].astype(BF16)

    def wait_rows(source, target, first_sem):
        most = pl.ds(0, (n_ent - 1) * blk)
        done = remote(source.at[most], target.at[most], first_sem, "ent", ent_peer(1))
        done.wait_recv()
        done.wait_send()

    def unpack(target):
        def body(k, carry):
            block = pl.ds(pl.multiple_of(k * blk, 16), blk)
            flat[block, :] = target[block, :].astype(F32)
            return carry

        lax.fori_loop(0, n_ent, body, 0)

    def slot_tile(j):
        return jnp.concatenate(
            [
                flat[pl.ds(2 * j, slots, stride=chunks), :],
                flat[pl.ds(2 * j + 1, slots, stride=chunks), :],
            ],
            axis=1,
        ).astype(BF16)

    send_rows(rep_send, rep_recv, 4)

    asked[...] = onehot(ask_row == iota((rows, slots), 0))
    pick_t[...] = onehot(slot_row == iota((slots, tri), 0))
    pick[...] = onehot(to_column(slot_row) == iota((tri, slots), 1))

    neg = neg_ref[...]
    neg_high = lax.shift_right_logical(neg, 7)
    neg_low = neg - neg_high * LANES
    counts = dot_nt(
        onehot(neg_high == iota((8, negs), 0)), onehot(neg_low == iota((LANES, negs), 0))
    )
    count[...] = jnp.concatenate([counts[v : v + 1, :] for v in range(rows // LANES)], axis=1)

    tail_row = tail_ref[...]
    tail_hot[...] = onehot(tail_row == iota((rows, tri), 0))
    tail_pick = onehot(to_column(tail_row) == iota((tri, rows), 1))

    def tails(j, square):
        columns = pl.ds(pl.multiple_of(j * tile, tile), tile)
        part = table[:, columns]
        parts = split3(part)
        positive[:, columns] = (
            dot(tail_pick, parts[2]) + dot(tail_pick, parts[1]) + dot(tail_pick, parts[0])
        )
        return square + jnp.sum(part * part, axis=1, keepdims=True)

    row_sq[...] = to_row(lax.fori_loop(0, tiles, tails, jnp.zeros((rows, 1), F32)))

    load_phase.wait()
    rel_pick = onehot(to_column(rel_ref[...]) == iota((tri, rels), 1))

    def angles(j, carry):
        columns = pl.ds(pl.multiple_of(j * LANES, LANES), LANES)
        parts = split3(phase[:, columns])
        angle = dot(rel_pick, parts[2]) + dot(rel_pick, parts[1]) + dot(rel_pick, parts[0])
        cosine[:, columns] = jnp.cos(angle)
        sine[:, columns] = jnp.sin(angle)
        return carry

    lax.fori_loop(0, half // LANES, angles, 0)
    state_col[...] = to_column(state_ref[...])

    wait_rows(rep_send, rep_recv, 4)
    unpack(rep_recv)

    def rotate(j, sums):
        sums_rot, sums_diff = sums
        re = pl.ds(pl.multiple_of(j * tile, tile), tile)
        im = pl.ds(pl.multiple_of(half + j * tile, tile), tile)
        head_re = dot(pick[...], slot_tile(j))
        head_im = dot(pick[...], slot_tile(j + tiles // 2))
        cos, sin = cosine[:, re], sine[:, re]
        rot_re = head_re * cos - head_im * sin
        rot_im = head_re * sin + head_im * cos
        rotated[:, re] = rot_re
        rotated[:, im] = rot_im
        diff_re = rot_re - positive[:, re]
        diff_im = rot_im - positive[:, im]
        sums_rot += jnp.sum(rot_re * rot_re + rot_im * rot_im, axis=1, keepdims=True)
        sums_diff += jnp.sum(diff_re * diff_re + diff_im * diff_im, axis=1, keepdims=True)
        return sums_rot, sums_diff

    nothing = jnp.zeros((tri, 1), F32)
    rot_sq, diff_sq = lax.fori_loop(0, tiles // 2, rotate, (nothing, nothing))
    rotated_bf = rotated[...].astype(BF16)
    scores = dot_nt(rotated_bf, table_bf[...])
    distance = (rot_sq + row_sq[...] - 2.0 * scores) * (1.0 / half)
    dist_pos = diff_sq * (1.0 / half)
    logits = MARGIN - distance
    times = count[...]
    named = times > 0.0
    masked = jnp.where(named, logits, -jnp.inf)
    shifted = times * jnp.exp(masked - jnp.max(masked, axis=1, keepdims=True))
    weights = shifted / jnp.sum(shifted, axis=1, keepdims=True)
    row_coef = -0.5 * weights * jax.nn.sigmoid(logits)
    pos_coef = 0.5 * jax.nn.sigmoid(dist_pos - MARGIN)
    row_coef_bf = row_coef.astype(BF16)
    total_coef = pos_coef + jnp.sum(row_coef, axis=1, keepdims=True)

    def head_grad(j, carry):
        re = pl.ds(pl.multiple_of(j * tile, tile), tile)
        im = pl.ds(pl.multiple_of(half + j * tile, tile), tile)
        out = []
        for columns in (re, im):
            pulled = dot(row_coef_bf, table_bf[:, columns])
            out.append(
                2.0
                / half
                * (total_coef * rotated[:, columns] - pos_coef * positive[:, columns] - pulled)
            )
        cos, sin = cosine[:, re], sine[:, re]
        grad_re = (out[0] * cos + out[1] * sin).astype(BF16)
        grad_im = (out[1] * cos - out[0] * sin).astype(BF16)
        for at, value in ((j, grad_re), (j + tiles // 2, grad_im)):
            part = dot(pick_t[...], value)
            flat[pl.ds(2 * at, slots, stride=chunks), :] = part[:, :LANES]
            flat[pl.ds(2 * at + 1, slots, stride=chunks), :] = part[:, LANES:]
        return carry

    lax.fori_loop(0, tiles // 2, head_grad, 0)
    send_rows(gr_send, gr_recv, 6)

    scale = 2.0 / half
    turned = jnp.transpose(row_coef)
    column = jnp.sum(turned, axis=1, keepdims=True) * scale
    turned_bf = turned.astype(BF16)
    pos_scaled = pos_coef * -scale

    def own_part(j, carry):
        columns = pl.ds(pl.multiple_of(j * tile, tile), tile)
        rot = rotated[:, columns]
        push = pos_scaled * (rot - positive[:, columns])
        push_high = push.astype(BF16)
        push_low = (push - push_high.astype(F32)).astype(BF16)
        partial[:, columns] = (
            column * table[:, columns]
            - scale * dot(turned_bf, rot.astype(BF16))
            + dot(tail_hot[...], push_high)
            + dot(tail_hot[...], push_low)
        )
        return carry

    lax.fori_loop(0, tiles, own_part, 0)

    wait_rows(gr_send, gr_recv, 6)
    unpack(gr_recv)

    theirs = pl.ds(pl.multiple_of((1 - core) * hrows, hrows), hrows)
    ours = pl.ds(pl.multiple_of(core * hrows, hrows), hrows)

    def add_theirs(j, carry):
        columns = pl.ds(pl.multiple_of(j * tile, tile), tile)
        pair_send[:, columns] = (
            partial[theirs, columns] + dot(asked[theirs, :], slot_tile(j))
        ).astype(BF16)
        return carry

    lax.fori_loop(0, tiles, add_theirs, 0)
    pair = remote(pair_send, pair_recv, 8, "dp", partner)
    pair.start()

    def add_ours(j, carry):
        columns = pl.ds(pl.multiple_of(j * tile, tile), tile)
        partial[ours, columns] += dot(asked[ours, :], slot_tile(j))
        return carry

    lax.fori_loop(0, tiles, add_ours, 0)
    pair.wait_recv()

    def piece_of(index):
        block = pl.ds(pl.multiple_of(index * prow, prow), prow)
        mine = pl.ds(pl.multiple_of(core * hrows + index * prow, prow), prow)
        return (partial[mine, :] + pair_recv[block, :].astype(F32)).astype(BF16)

    def send_piece(k, carry):
        to = z_peer(k)
        z_send[to] = piece_of(to)
        remote(z_send.at[to], z_recv.at[z], 10, "dp", 2 * to + core).start()
        return carry

    lax.fori_loop(1, nz, send_piece, 0)
    z_recv[z] = piece_of(z)
    pieces = remote(z_send.at[pl.ds(0, nz - 1)], z_recv.at[pl.ds(0, nz - 1)], 10, "dp", partner)
    pieces.wait_recv()

    def add_piece(k, value):
        return value + z_recv[k].astype(F32)

    here = pl.ds(pl.multiple_of(core * hrows + z * prow, prow), prow)
    total[here, :] = lax.fori_loop(1, nz, add_piece, z_recv[0].astype(F32)).astype(BF16)

    def send_total(k, carry):
        remote(total.at[here], total.at[here], 12, "dp", 2 * z_peer(k) + core).start()
        return carry

    lax.fori_loop(1, nz, send_total, 0)
    most = pl.ds(0, (nz - 1) * prow)
    spread = remote(total.at[most], total.at[most], 12, "dp", partner)
    spread.wait_recv()
    swap = remote(total.at[ours], total.at[ours], 14, "dp", partner)
    swap.start()

    def update(first_row):
        def body(k, carry):
            block = pl.ds(pl.multiple_of(first_row + k * 32, 32), 32)
            value = total[block, :].astype(F32)
            new = state_col[block, :] + jnp.sum(value * value, axis=1, keepdims=True) / width
            state_col[block, :] = new
            out_table[block, :] = table[block, :] - value * (LEARN_RATE / jnp.sqrt(new))
            return carry

        lax.fori_loop(0, hrows // 32, body, 0)

    update(core * hrows)
    swap.wait_recv()
    update((1 - core) * hrows)
    out_state[...] = to_row(state_col[...])
    pair.wait_send()
    pieces.wait_send()
    spread.wait_send()
    swap.wait_send()


def on_device(
    n_ent,
    n_dp,
    entity_table,
    adagrad_state,
    relation_phase,
    head_owner,
    head_row,
    relation_id,
    tail_row,
    negative_row,
):
    rows, width = entity_table.shape
    rels, half = relation_phase.shape
    tri = head_row.shape[0]
    negs = negative_row.shape[0]
    cap = 12
    slots = n_ent * cap
    chunks = width // LANES
    hrows = rows // 2
    prow = rows // n_dp
    nz = n_dp // 2
    vmem = pl.BlockSpec(memory_space=pltpu.VMEM)
    anywhere = pl.BlockSpec(memory_space=pl.ANY)
    new_table, new_state = pl.pallas_call(
        functools.partial(kernel, n_ent, n_dp, cap),
        out_shape=(
            jax.ShapeDtypeStruct((rows, width), F32),
            jax.ShapeDtypeStruct((1, rows), F32),
        ),
        in_specs=[anywhere, vmem, anywhere, vmem, vmem, vmem, vmem, vmem],
        out_specs=(vmem, vmem),
        scratch_shapes=[
            pltpu.VMEM((rows, width), F32),
            pltpu.VMEM((rows, width), BF16),
            pltpu.VMEM((rels, half), F32),
            pltpu.VMEM((slots * chunks, LANES), F32),
            pltpu.VMEM((n_ent, 1, LANES), F32),
            pltpu.VMEM((n_ent, 1, LANES), F32),
            pltpu.VMEM((slots * chunks, LANES), BF16),
            pltpu.VMEM((slots * chunks, LANES), BF16),
            pltpu.VMEM((slots * chunks, LANES), BF16),
            pltpu.VMEM((slots * chunks, LANES), BF16),
            pltpu.VMEM((tri, slots), BF16),
            pltpu.VMEM((slots, tri), BF16),
            pltpu.VMEM((rows, slots), BF16),
            pltpu.VMEM((slots, rows), BF16),
            pltpu.VMEM((rows, tri), BF16),
            pltpu.VMEM((1, rows), F32),
            pltpu.VMEM((1, rows), F32),
            pltpu.VMEM((tri, width), F32),
            pltpu.VMEM((tri, half), F32),
            pltpu.VMEM((tri, half), F32),
            pltpu.VMEM((tri, width), F32),
            pltpu.VMEM((rows, width), F32),
            pltpu.VMEM((hrows, width), BF16),
            pltpu.VMEM((hrows, width), BF16),
            pltpu.VMEM((nz, prow, width), BF16),
            pltpu.VMEM((nz, prow, width), BF16),
            pltpu.VMEM((rows, width), BF16),
            pltpu.VMEM((rows, 1), F32),
            pltpu.SemaphoreType.DMA((16,)),
        ],
        compiler_params=pltpu.CompilerParams(
            collective_id=0, has_side_effects=True, vmem_limit_bytes=48 * 1024 * 1024
        ),
    )(
        entity_table,
        adagrad_state.reshape(1, rows),
        relation_phase,
        head_owner.reshape(1, tri),
        head_row.reshape(1, tri),
        relation_id.reshape(1, tri),
        tail_row.reshape(1, tri),
        negative_row.reshape(1, negs),
    )
    return new_table, new_state.reshape(rows)


def solution(mesh):
    return jax.shard_map(
        functools.partial(on_device, mesh.shape["ent"], mesh.shape["dp"]),
        mesh=mesh,
        in_specs=(
            P("ent", None),
            P("ent"),
            P(),
            P(("dp", "ent"), None),
            P(("dp", "ent")),
            P(("dp", "ent")),
            P(("dp", "ent")),
            P(("dp", "ent")),
        ),
        out_specs=(P("ent", None), P("ent")),
        check_vma=False,
    )
```

time: 268 us -> 107 us (0.40)
  waiting for transfers between devices: 148 us -> 0 us
  Pallas kernels: 0 us -> 97.6 us
  other arithmetic: 40.9 us -> 0 us
  starting transfers between devices: 24.6 us -> 0 us
  local copies, waits for them, and re-layouts: 27.9 us -> 8.66 us
  between operations: 14.3 us -> 0.66 us
  matrix products: 12.2 us -> 0 us
    psum x1 -> x0, waiting for transfers between devices: 122 us -> none  [on_device(): summed = lax.psum(local_grad.astype(jnp.bfloat16), 'dp').astype(jnp.float32)]
    pallas_call x0 -> x1, Pallas kernels: none -> 97.6 us  [on_device(): pl.pallas_call(functools.partial(kernel, n_ent, n_dp, cap), out_shape=(ja...]
    all_to_all x3 -> x0, waiting for transfers between devices: 26.1 us -> none  [the longest x1 13.9 us: on_device(): lax.all_to_all(outgoing.astype(jnp.bfloat16), 'ent', split_axis=0, concat...]
    all_to_all x3 -> x0, starting transfers between devices: 24.5 us -> none  [the longest x1 10.5 us: on_device(): lax.all_to_all(requests, 'ent', split_axis=0, concat_axis=0, tiled=True)]
    gather x6 -> x0, local copies, waits for them, and re-layouts: 18 us -> none  [the longest x1 9.67 us: on_device(): negative_bf = jnp.take(table_bf, negative_row, axis=0)]
    dot_general x5 -> x0, matrix products: 12.2 us -> none  [the longest x1 3.65 us: on_device(): jnp.dot(rotated_bf, negative_bf.T, preferred_element_type=jnp.float32)]
    scatter-add x2 -> x0, other arithmetic: 11 us -> none  [the longest x1 5.9 us: on_device(): jax.ops.segment_sum(incoming.reshape(owners * capacity, 2 * half), asked_...]
    unnamed x38 -> x18, local copies, waits for them, and re-layouts: 0.71 us -> 8.66 us
  transfers between devices with their start and end apart: 4 -> 0, of which waited for: 4 -> 0; matrix products, arithmetic and copies ran while one was open for 12% -> 0% of each run, Pallas kernels for 0% -> 0%
where the time goes in v1:
time: 107 us
  Pallas kernels  97.6 us (91%)
  local copies, waits for them, and re-layouts  8.66 us (8%)
    pallas_call x1, Pallas kernels, on_device(): pl.pallas_call(functools.partial(kernel, n_ent, n_dp, cap), out_shape=(ja...  97.6 us
    unnamed x18, local copies, waits for them, and re-layouts  8.66 us

profile of v1, /device:TPU:1, one launch (start us, length us, event | category | flops | bytes accessed | tf_op | source)
XLA Modules:
  0.0 107.0 jit_solution(4785112364703029973)
XLA Ops:
  0.6 0.0 copy-start
  0.6 1.6 %copy-done = f32[512,1024]{1,0:T(8,128)S(1)} copy-done((f32[512,1024]{1,0:T(8,128)S(1)}, f32[512,1024]{1,0:T(8,128)}, u32[]{:S(2)}) %copy-start) | copy-done | bytes 2097176
  2.2 0.0 copy-start.1
  2.2 1.2 %copy-done.1 = f32[448,512]{1,0:T(8,128)S(1)} copy-done((f32[448,512]{1,0:T(8,128)S(1)}, f32[448,512]{1,0:T(8,128)}, u32[]{:S(2)}) %copy-start.1) | copy-done | bytes 917528
  3.4 0.0 copy-start.2
  3.4 0.7 copy-done.2
  4.1 0.0 copy-start.3
  4.1 0.7 copy-done.3
  4.8 0.0 copy-start.4
  4.8 0.7 copy-done.4
  5.4 0.0 copy-start.5
  5.4 0.7 copy-done.5
  6.1 0.0 copy-start.6
  6.1 0.7 copy-done.6
  6.8 0.0 copy-start.7
  6.8 0.7 copy-done.7
  7.4 97.6 %shard_map.95 = (f32[512,1024]{1,0:T(8,128)S(1)}, f32[1,512]{1,0:T(1,128)S(1)}) custom-call(f32[512,1024]{1,0:T(8,128)S(1)} %copy-done, f32[1,512]{1,0:T(1,128)S(1)} %bitcast.9, f32[448,512]{1,0:T(8,128)S(1)} %copy-done.1, s32[1,128]{1,0:T(1,128)S(1)} %bitcast.10, s32[1,128]{1,0:T(1,128)S(1)} %bitcast.11, s32[1,128]{1,0:T(1,128)S(1)} %bitcast.12, ...), custom_call_target="tpu_custom_call" | custom-call | tf_op jit(solution)/shard_map/pallas_call | solution.py:505
  105.1 1.3 %copy.12 = f32[512,1024]{1,0:T(8,128)} copy(f32[512,1024]{1,0:T(8,128)S(1)} %get-tuple-element.8) | data formatting | bytes 4194304
  106.4 0.6 copy.13
Async XLA Ops:
  0.6 1.6 %copy-start = (f32[512,1024]{1,0:T(8,128)S(1)}, f32[512,1024]{1,0:T(8,128)}, u32[]{:S(2)}) copy-start(f32[512,1024]{1,0:T(8,128)} %table_hbm.1) | copy-start | bytes 6291460
  2.2 1.2 %copy-start.1 = (f32[448,512]{1,0:T(8,128)S(1)}, f32[448,512]{1,0:T(8,128)}, u32[]{:S(2)}) copy-start(f32[448,512]{1,0:T(8,128)} %phase_hbm.1) | copy-start | bytes 2752516
  3.4 0.7 copy-start.2
  4.1 0.7 copy-start.3
  4.8 0.7 copy-start.4
  5.4 0.7 copy-start.5
  6.1 0.7 copy-start.6
  6.8 0.7 copy-start.7

commit v2 on v1

--- a/solution.py
+++ b/solution.py
@@ -55,18 +55,24 @@
     n_dp,
     cap,
     table_hbm,
+    state_hbm,
+    phase_hbm,
+    owner_hbm,
+    hrow_hbm,
+    rel_hbm,
+    tail_hbm,
+    neg_hbm,
+    out_table,
+    out_state,
+    table,
+    table_bf,
+    phase,
     state_ref,
-    phase_hbm,
     owner_ref,
     hrow_ref,
     rel_ref,
     tail_ref,
     neg_ref,
-    out_table,
-    out_state,
-    table,
-    table_bf,
-    phase,
     flat,
     req_send,
     req_recv,
@@ -88,14 +94,20 @@
     partial,
     pair_send,
     pair_recv,
-    z_send,
-    z_recv,
+    ring_send,
+    ring_recv,
     total,
     state_col,
+    gr_flat_0,
+    gr_flat_1,
     sems,
+    load_sems,
+    ring_sems,
+    spread_sems,
 ):
     rows, width = table.shape
     half = width // 2
+    gr_flat = (gr_flat_0, gr_flat_1)
     tri = hrow_ref.shape[1]
     negs = neg_ref.shape[1]
     rels = phase.shape[0]
@@ -118,56 +130,58 @@
     x = lax.rem(ent, nx)
     partner = dp + 1 - 2 * core
 
-    def turn(m, n):
-        odd = lax.rem(m, 2)
-        return lax.rem((2 * odd - 1) * lax.div(m + 1, 2) + n, n)
+    def shift(m, n):
+        return ((m + 1) // 2 if m % 2 else -(m // 2)) % n
 
     def ent_peer(k):
-        dy = turn(lax.rem(k, ny), ny)
-        dx = lax.div(k, ny)
-        return lax.rem(y + dy, ny) * nx + lax.rem(x + dx, nx)
+        return lax.rem(y + shift(k % ny, ny), ny) * nx + lax.rem(x + k // ny, nx)
 
     def z_peer(k):
-        return lax.rem(z + turn(nz - k, nz), nz)
-
-    def remote(src, dst, first_sem, axis, index):
+        return lax.rem(z + shift(nz - k, nz), nz)
+
+    def remote(src, dst, send_sem, recv_sem, axis, index):
         return pltpu.make_async_remote_copy(
             src_ref=src,
             dst_ref=dst,
-            send_sem=sems.at[first_sem],
-            recv_sem=sems.at[first_sem + 1],
+            send_sem=send_sem,
+            recv_sem=recv_sem,
             device_id={axis: index},
             device_id_type=pl.DeviceIdType.MESH,
         )
 
-    load_table = pltpu.make_async_copy(table_hbm, table, sems.at[0])
-    load_phase = pltpu.make_async_copy(phase_hbm, phase, sems.at[1])
-    load_table.start()
-    load_phase.start()
+    loads = [
+        pltpu.make_async_copy(source, target, load_sems.at[i])
+        for i, (source, target) in enumerate(
+            (
+                (owner_hbm, owner_ref),
+                (hrow_hbm, hrow_ref),
+                (table_hbm, table),
+                (tail_hbm, tail_ref),
+                (rel_hbm, rel_ref),
+                (neg_hbm, neg_ref),
+                (state_hbm, state_ref),
+                (phase_hbm, phase),
+            )
+        )
+    ]
+    for load in loads:
+        load.start()
 
     barrier = pltpu.get_barrier_semaphore()
 
-    def greet_ent(k, carry):
+    def greet(axis, index):
         pl.semaphore_signal(
-            barrier, inc=1, device_id={"ent": ent_peer(k)}, device_id_type=pl.DeviceIdType.MESH
-        )
-        return carry
-
-    def greet_z(k, carry):
-        pl.semaphore_signal(
-            barrier,
-            inc=1,
-            device_id={"dp": 2 * z_peer(k) + core},
-            device_id_type=pl.DeviceIdType.MESH,
-        )
-        return carry
-
-    lax.fori_loop(1, n_ent, greet_ent, 0)
-    lax.fori_loop(1, nz, greet_z, 0)
-    pl.semaphore_signal(
-        barrier, inc=1, device_id={"dp": partner}, device_id_type=pl.DeviceIdType.MESH
-    )
-
+            barrier, inc=1, device_id={axis: index}, device_id_type=pl.DeviceIdType.MESH
+        )
+
+    for k in range(1, n_ent):
+        greet("ent", ent_peer(k))
+    for k in range(1, nz):
+        greet("dp", 2 * z_peer(k) + core)
+    greet("dp", partner)
+
+    loads[0].wait()
+    loads[1].wait()
     owner_row = owner_ref[...]
     own_hot = owner_row == iota((n_ent, tri), 0)
     own_bf = onehot(own_hot)
@@ -188,15 +202,12 @@
 
     pl.semaphore_wait(barrier, n_ent - 1 + nz - 1 + 1)
 
-    def send_request(k, carry):
+    for k in range(1, n_ent):
         q = ent_peer(k)
-        remote(req_send.at[q], req_recv.at[ent], 2, "ent", q).start()
-        return carry
-
-    lax.fori_loop(1, n_ent, send_request, 0)
+        remote(req_send.at[q], req_recv.at[ent], sems.at[0], sems.at[1], "ent", q).start()
     req_recv[ent] = req_send[ent]
 
-    load_table.wait()
+    loads[2].wait()
 
     def cast_table(j, carry):
         columns = pl.ds(pl.multiple_of(j * tile, tile), tile)
@@ -205,8 +216,9 @@
 
     lax.fori_loop(0, tiles, cast_table, 0)
 
+    most = pl.ds(0, n_ent - 1)
     got = remote(
-        req_send.at[pl.ds(0, n_ent - 1)], req_recv.at[pl.ds(0, n_ent - 1)], 2, "ent", ent_peer(1)
+        req_send.at[most], req_recv.at[most], sems.at[0], sems.at[1], "ent", ent_peer(1)
     )
     got.wait_recv()
     got.wait_send()
@@ -233,34 +245,32 @@
 
     lax.fori_loop(0, tiles, fetch, 0)
 
-    def send_rows(source, target, first_sem):
-        def body(k, carry):
+    def send_rows(buffer, source, target, sem):
+        size = buffer.shape[0] // n_ent
+        own = pl.ds(pl.multiple_of(ent * size, 16), size)
+        for k in range(1, n_ent):
             q = ent_peer(k)
-            block = pl.ds(pl.multiple_of(q * blk, 16), blk)
-            source[block, :] = flat[block, :].astype(BF16)
+            block = pl.ds(pl.multiple_of(q * size, 16), size)
+            source[block, :] = buffer[block, :].astype(BF16)
             remote(
-                source.at[block],
-                target.at[pl.ds(pl.multiple_of(ent * blk, 16), blk)],
-                first_sem,
-                "ent",
-                q,
+                source.at[block], target.at[own], sems.at[sem], sems.at[sem + 1], "ent", q
             ).start()
-            return carry
-
-        lax.fori_loop(1, n_ent, body, 0)
-        own = pl.ds(pl.multiple_of(ent * blk, 16), blk)
-        target[own, :] = flat[own, :].astype(BF16)
-
-    def wait_rows(source, target, first_sem):
-        most = pl.ds(0, (n_ent - 1) * blk)
-        done = remote(source.at[most], target.at[most], first_sem, "ent", ent_peer(1))
+        target[own, :] = buffer[own, :].astype(BF16)
+
+    def wait_rows(source, target, sem):
+        most = pl.ds(0, target.shape[0] // n_ent * (n_ent - 1))
+        done = remote(
+            source.at[most], target.at[most], sems.at[sem], sems.at[sem + 1], "ent", ent_peer(1)
+        )
         done.wait_recv()
         done.wait_send()
 
-    def unpack(target):
+    def unpack(target, buffer):
+        size = buffer.shape[0] // n_ent
+
         def body(k, carry):
-            block = pl.ds(pl.multiple_of(k * blk, 16), blk)
-            flat[block, :] = target[block, :].astype(F32)
+            block = pl.ds(pl.multiple_of(k * size, 16), size)
+            buffer[block, :] = target[block, :].astype(F32)
             return carry
 
         lax.fori_loop(0, n_ent, body, 0)
@@ -274,8 +284,10 @@
             axis=1,
         ).astype(BF16)
 
-    send_rows(rep_send, rep_recv, 4)
-
+    send_rows(flat, rep_send, rep_recv, 2)
+
+    for load in loads[3:]:
+        load.wait()
     asked[...] = onehot(ask_row == iota((rows, slots), 0))
     pick_t[...] = onehot(slot_row == iota((slots, tri), 0))
     pick[...] = onehot(to_column(slot_row) == iota((tri, slots), 1))
@@ -303,7 +315,6 @@
 
     row_sq[...] = to_row(lax.fori_loop(0, tiles, tails, jnp.zeros((rows, 1), F32)))
 
-    load_phase.wait()
     rel_pick = onehot(to_column(rel_ref[...]) == iota((tri, rels), 1))
 
     def angles(j, carry):
@@ -317,8 +328,8 @@
     lax.fori_loop(0, half // LANES, angles, 0)
     state_col[...] = to_column(state_ref[...])
 
-    wait_rows(rep_send, rep_recv, 4)
-    unpack(rep_recv)
+    wait_rows(rep_send, rep_recv, 2)
+    unpack(rep_recv, flat)
 
     def rotate(j, sums):
         sums_rot, sums_diff = sums
@@ -354,9 +365,10 @@
     row_coef_bf = row_coef.astype(BF16)
     total_coef = pos_coef + jnp.sum(row_coef, axis=1, keepdims=True)
 
-    def head_grad(j, carry):
-        re = pl.ds(pl.multiple_of(j * tile, tile), tile)
-        im = pl.ds(pl.multiple_of(half + j * tile, tile), tile)
+    quarter = half // 2
+    for h in range(2):
+        re = pl.ds(h * quarter, quarter)
+        im = pl.ds(half + h * quarter, quarter)
         out = []
         for columns in (re, im):
             pulled = dot(row_coef_bf, table_bf[:, columns])
@@ -368,14 +380,11 @@
         cos, sin = cosine[:, re], sine[:, re]
         grad_re = (out[0] * cos + out[1] * sin).astype(BF16)
         grad_im = (out[1] * cos - out[0] * sin).astype(BF16)
-        for at, value in ((j, grad_re), (j + tiles // 2, grad_im)):
+        for at, value in ((0, grad_re), (2, grad_im)):
             part = dot(pick_t[...], value)
-            flat[pl.ds(2 * at, slots, stride=chunks), :] = part[:, :LANES]
-            flat[pl.ds(2 * at + 1, slots, stride=chunks), :] = part[:, LANES:]
-        return carry
-
-    lax.fori_loop(0, tiles // 2, head_grad, 0)
-    send_rows(gr_send, gr_recv, 6)
+            gr_flat[h][pl.ds(at, slots, stride=4), :] = part[:, :LANES]
+            gr_flat[h][pl.ds(at + 1, slots, stride=4), :] = part[:, LANES:]
+        send_rows(gr_flat[h], gr_send.at[h], gr_recv.at[h], 4 + 2 * h)
 
     scale = 2.0 / half
     turned = jnp.transpose(row_coef)
@@ -383,99 +392,168 @@
     turned_bf = turned.astype(BF16)
     pos_scaled = pos_coef * -scale
 
-    def own_part(j, carry):
-        columns = pl.ds(pl.multiple_of(j * tile, tile), tile)
-        rot = rotated[:, columns]
-        push = pos_scaled * (rot - positive[:, columns])
-        push_high = push.astype(BF16)
-        push_low = (push - push_high.astype(F32)).astype(BF16)
-        partial[:, columns] = (
-            column * table[:, columns]
-            - scale * dot(turned_bf, rot.astype(BF16))
-            + dot(tail_hot[...], push_high)
-            + dot(tail_hot[...], push_low)
-        )
-        return carry
-
-    lax.fori_loop(0, tiles, own_part, 0)
-
-    wait_rows(gr_send, gr_recv, 6)
-    unpack(gr_recv)
+    def own_part(h):
+        def body(part, carry):
+            columns = pl.ds(pl.multiple_of(part * half + h * quarter, quarter), quarter)
+            rot = rotated[:, columns]
+            push = pos_scaled * (rot - positive[:, columns])
+            push_high = push.astype(BF16)
+            push_low = (push - push_high.astype(F32)).astype(BF16)
+            partial[h, :, pl.ds(pl.multiple_of(part * quarter, quarter), quarter)] = (
+                column * table[:, columns]
+                - scale * dot(turned_bf, rot.astype(BF16))
+                + dot(tail_hot[...], push_high)
+                + dot(tail_hot[...], push_low)
+            )
+            return carry
+
+        lax.fori_loop(0, 2, body, 0)
 
     theirs = pl.ds(pl.multiple_of((1 - core) * hrows, hrows), hrows)
     ours = pl.ds(pl.multiple_of(core * hrows, hrows), hrows)
-
-    def add_theirs(j, carry):
-        columns = pl.ds(pl.multiple_of(j * tile, tile), tile)
-        pair_send[:, columns] = (
-            partial[theirs, columns] + dot(asked[theirs, :], slot_tile(j))
-        ).astype(BF16)
-        return carry
-
-    lax.fori_loop(0, tiles, add_theirs, 0)
-    pair = remote(pair_send, pair_recv, 8, "dp", partner)
-    pair.start()
-
-    def add_ours(j, carry):
-        columns = pl.ds(pl.multiple_of(j * tile, tile), tile)
-        partial[ours, columns] += dot(asked[ours, :], slot_tile(j))
-        return carry
-
-    lax.fori_loop(0, tiles, add_ours, 0)
-    pair.wait_recv()
-
-    def piece_of(index):
-        block = pl.ds(pl.multiple_of(index * prow, prow), prow)
-        mine = pl.ds(pl.multiple_of(core * hrows + index * prow, prow), prow)
-        return (partial[mine, :] + pair_recv[block, :].astype(F32)).astype(BF16)
-
-    def send_piece(k, carry):
-        to = z_peer(k)
-        z_send[to] = piece_of(to)
-        remote(z_send.at[to], z_recv.at[z], 10, "dp", 2 * to + core).start()
-        return carry
-
-    lax.fori_loop(1, nz, send_piece, 0)
-    z_recv[z] = piece_of(z)
-    pieces = remote(z_send.at[pl.ds(0, nz - 1)], z_recv.at[pl.ds(0, nz - 1)], 10, "dp", partner)
-    pieces.wait_recv()
-
-    def add_piece(k, value):
-        return value + z_recv[k].astype(F32)
-
-    here = pl.ds(pl.multiple_of(core * hrows + z * prow, prow), prow)
-    total[here, :] = lax.fori_loop(1, nz, add_piece, z_recv[0].astype(F32)).astype(BF16)
-
-    def send_total(k, carry):
-        remote(total.at[here], total.at[here], 12, "dp", 2 * z_peer(k) + core).start()
-        return carry
-
-    lax.fori_loop(1, nz, send_total, 0)
-    most = pl.ds(0, (nz - 1) * prow)
-    spread = remote(total.at[most], total.at[most], 12, "dp", partner)
-    spread.wait_recv()
-    swap = remote(total.at[ours], total.at[ours], 14, "dp", partner)
-    swap.start()
+    longer, shorter = nz // 2, nz - 1 - nz // 2
+
+    def rows_of(index):
+        return pl.ds(pl.multiple_of(core * hrows + index * prow, prow), prow)
+
+    def ways(h):
+        lengths = (longer, shorter) if h == 0 else (shorter, longer)
+        return [(w, (1, -1)[w], lengths[w]) for w in range(2) if lengths[w] > 0]
+
+    def chip(distance):
+        return lax.rem(z + distance + 2 * nz, nz)
+
+    def add_incoming(h, some):
+        def body(part, carry):
+            columns = pl.ds(pl.multiple_of(part * quarter, quarter), quarter)
+            value = jnp.concatenate(
+                [
+                    gr_flat[h][pl.ds(2 * part, slots, stride=4), :],
+                    gr_flat[h][pl.ds(2 * part + 1, slots, stride=4), :],
+                ],
+                axis=1,
+            ).astype(BF16)
+            sums = partial[h, some, columns] + dot(asked[some, :], value)
+            if some is theirs:
+                pair_send[h, :, columns] = sums.astype(BF16)
+            else:
+                partial[h, some, columns] = sums
+            return carry
+
+        lax.fori_loop(0, 2, body, 0)
+
+    def pair(h):
+        return remote(
+            pair_send.at[h], pair_recv.at[h], sems.at[8 + 2 * h], sems.at[9 + 2 * h], "dp", partner
+        )
+
+    def collect(h):
+        wait_rows(gr_send.at[h], gr_recv.at[h], 4 + 2 * h)
+        unpack(gr_recv.at[h], gr_flat[h])
+        add_incoming(h, theirs)
+        pair(h).start()
+        add_incoming(h, ours)
+
+    def take_pair(h):
+        pair(h).wait_recv()
+        partial[h, ours, :] += pair_recv[h].astype(F32)
+
+    def ring(h, w, step, hop):
+        return remote(
+            ring_send.at[h, w, hop - 1],
+            ring_recv.at[h, w, hop - 1],
+            sems.at[12 + h],
+            ring_sems.at[h, w, hop - 1],
+            "dp",
+            2 * chip(step) + core,
+        )
+
+    def sum_hop(h, hop):
+        for w, step, length in ways(h):
+            if hop <= length:
+                value = partial[h, rows_of(chip(step * (length - hop + 1))), :]
+                if hop > 1:
+                    ring(h, w, step, hop - 1).wait_recv()
+                    value += ring_recv[h, w, hop - 2].astype(F32)
+                ring_send[h, w, hop - 1] = value.astype(BF16)
+                ring(h, w, step, hop).start()
+
+    def sum_end(h):
+        value = partial[h, rows_of(z), :]
+        for w, step, length in ways(h):
+            ring(h, w, step, length).wait_recv()
+            value += ring_recv[h, w, length - 1].astype(F32)
+        total[h, rows_of(z), :] = value.astype(BF16)
+
+    def spread(h, w, step, hop):
+        piece = total.at[h, rows_of(chip(-step * (hop - 1)))]
+        return remote(
+            piece, piece, sems.at[14 + h], spread_sems.at[h, w, hop - 1], "dp", 2 * chip(step) + core
+        )
+
+    def across(h, piece):
+        return remote(piece, piece, sems.at[16 + 2 * h], sems.at[17 + 2 * h], "dp", partner)
+
+    def spread_hop(h, hop):
+        if hop == 1:
+            for w, step, length in ways(h):
+                spread(h, w, step, 1).start()
+            across(h, total.at[h, rows_of(z)]).start()
+            return
+        for w, step, length in ways(h):
+            if hop <= length + 1:
+                spread(h, w, step, hop - 1).wait_recv()
+                if hop <= length:
+                    spread(h, w, step, hop).start()
+                across(h, total.at[h, rows_of(chip(-step * (hop - 1)))]).start()
+
+    hops = longer
+    own_part(0)
+    own_part(1)
+    collect(0)
+    take_pair(0)
+    for hop in range(1, hops + 1):
+        sum_hop(0, hop)
+    sum_end(0)
+    spread_hop(0, 1)
+    collect(1)
+    take_pair(1)
+    for hop in range(1, hops + 1):
+        sum_hop(1, hop)
+        spread_hop(0, hop + 1)
+    sum_end(1)
+    for hop in range(1, hops + 2):
+        spread_hop(1, hop)
 
     def update(first_row):
         def body(k, carry):
             block = pl.ds(pl.multiple_of(first_row + k * 32, 32), 32)
-            value = total[block, :].astype(F32)
-            new = state_col[block, :] + jnp.sum(value * value, axis=1, keepdims=True) / width
+            values = [total[h, block, :].astype(F32) for h in range(2)]
+            square = values[0] * values[0] + values[1] * values[1]
+            new = state_col[block, :] + jnp.sum(square, axis=1, keepdims=True) / width
             state_col[block, :] = new
-            out_table[block, :] = table[block, :] - value * (LEARN_RATE / jnp.sqrt(new))
+            rate = LEARN_RATE / jnp.sqrt(new)
+            for h in range(2):
+                for part in range(2):
+                    columns = pl.ds(part * half + h * quarter, quarter)
+                    value = values[h][:, part * quarter : (part + 1) * quarter]
+                    out_table[block, columns] = table[block, columns] - value * rate
             return carry
 
         lax.fori_loop(0, hrows // 32, body, 0)
 
     update(core * hrows)
-    swap.wait_recv()
+    for h in range(2):
+        across(h, total.at[h, theirs]).wait_recv()
     update((1 - core) * hrows)
     out_state[...] = to_row(state_col[...])
-    pair.wait_send()
-    pieces.wait_send()
-    spread.wait_send()
-    swap.wait_send()
+    for h in range(2):
+        pair(h).wait_send()
+        pieces = pl.ds(0, (nz - 1) * prow)
+        piece = total.at[h, pieces]
+        remote(piece, piece, sems.at[12 + h], sems.at[12 + h], "dp", partner).wait_send()
+        remote(piece, piece, sems.at[14 + h], sems.at[14 + h], "dp", partner).wait_send()
+        across(h, total.at[h, ours]).wait_send()
 
 
 def on_device(
@@ -501,26 +579,32 @@
     prow = rows // n_dp
     nz = n_dp // 2
     vmem = pl.BlockSpec(memory_space=pltpu.VMEM)
-    anywhere = pl.BlockSpec(memory_space=pl.ANY)
+    hbm = pl.BlockSpec(memory_space=pltpu.HBM)
     new_table, new_state = pl.pallas_call(
         functools.partial(kernel, n_ent, n_dp, cap),
         out_shape=(
             jax.ShapeDtypeStruct((rows, width), F32),
             jax.ShapeDtypeStruct((1, rows), F32),
         ),
-        in_specs=[anywhere, vmem, anywhere, vmem, vmem, vmem, vmem, vmem],
+        in_specs=[hbm] * 8,
         out_specs=(vmem, vmem),
         scratch_shapes=[
             pltpu.VMEM((rows, width), F32),
             pltpu.VMEM((rows, width), BF16),
             pltpu.VMEM((rels, half), F32),
+            pltpu.VMEM((1, rows), F32),
+            pltpu.VMEM((1, tri), jnp.int32),
+            pltpu.VMEM((1, tri), jnp.int32),
+            pltpu.VMEM((1, tri), jnp.int32),
+            pltpu.VMEM((1, tri), jnp.int32),
+            pltpu.VMEM((1, negs), jnp.int32),
             pltpu.VMEM((slots * chunks, LANES), F32),
             pltpu.VMEM((n_ent, 1, LANES), F32),
             pltpu.VMEM((n_ent, 1, LANES), F32),
             pltpu.VMEM((slots * chunks, LANES), BF16),
             pltpu.VMEM((slots * chunks, LANES), BF16),
-            pltpu.VMEM((slots * chunks, LANES), BF16),
-            pltpu.VMEM((slots * chunks, LANES), BF16),
+            pltpu.VMEM((2, slots * chunks // 2, LANES), BF16),
+            pltpu.VMEM((2, slots * chunks // 2, LANES), BF16),
             pltpu.VMEM((tri, slots), BF16),
             pltpu.VMEM((slots, tri), BF16),
             pltpu.VMEM((rows, slots), BF16),
@@ -532,19 +616,24 @@
             pltpu.VMEM((tri, half), F32),
             pltpu.VMEM((tri, half), F32),
             pltpu.VMEM((tri, width), F32),
-            pltpu.VMEM((rows, width), F32),
-            pltpu.VMEM((hrows, width), BF16),
-            pltpu.VMEM((hrows, width), BF16),
-            pltpu.VMEM((nz, prow, width), BF16),
-            pltpu.VMEM((nz, prow, width), BF16),
-            pltpu.VMEM((rows, width), BF16),
+            pltpu.VMEM((2, rows, half), F32),
+            pltpu.VMEM((2, hrows, half), BF16),
+            pltpu.VMEM((2, hrows, half), BF16),
+            pltpu.VMEM((2, 2, nz // 2, prow, half), BF16),
+            pltpu.VMEM((2, 2, nz // 2, prow, half), BF16),
+            pltpu.VMEM((2, rows, half), BF16),
             pltpu.VMEM((rows, 1), F32),
-            pltpu.SemaphoreType.DMA((16,)),
+            pltpu.VMEM((slots * chunks // 2, LANES), F32),
+            pltpu.VMEM((slots * chunks // 2, LANES), F32),
+            pltpu.SemaphoreType.DMA((20,)),
+            pltpu.SemaphoreType.DMA((8,)),
+            pltpu.SemaphoreType.DMA((2, 2, nz // 2)),
+            pltpu.SemaphoreType.DMA((2, 2, nz // 2)),
         ],
         compiler_params=pltpu.CompilerParams(
             collective_id=0, has_side_effects=True, vmem_limit_bytes=48 * 1024 * 1024
         ),
-    )(
+    )(*[pltpu.with_memory_space_constraint(a, pltpu.HBM) for a in (
         entity_table,
         adagrad_state.reshape(1, rows),
         relation_phase,
@@ -553,7 +642,7 @@
         relation_id.reshape(1, tri),
         tail_row.reshape(1, tri),
         negative_row.reshape(1, negs),
-    )
+    )])
     return new_table, new_state.reshape(rows)
 
 

time: 107 us -> 105 us (0.981)
  local copies, waits for them, and re-layouts: 8.66 us -> 1.9 us
  Pallas kernels: 97.6 us -> 102 us
    unnamed x18 -> x2, local copies, waits for them, and re-layouts: 8.66 us -> 1.9 us
    pallas_call x1, Pallas kernels: 97.6 us -> 102 us  [on_device(): pl.pallas_call(functools.partial(kernel, n_ent, n_dp, cap), out_shape=(ja...]
where the time goes in v2:
time: 105 us
  Pallas kernels  102 us (97%)
  local copies, waits for them, and re-layouts  1.9 us (2%)
    pallas_call x1, Pallas kernels, on_device(): pl.pallas_call(functools.partial(kernel, n_ent, n_dp, cap), out_shape=(ja...  102 us

profile of v2, /device:TPU:1, one launch (start us, length us, event | category | flops | bytes accessed | tf_op | source)
XLA Modules:
  0.0 104.6 jit_solution(9948251783571018750)
XLA Ops:
  0.6 102.0 %shard_map.95 = (f32[512,1024]{1,0:T(8,128)S(1)}, f32[1,512]{1,0:T(1,128)S(1)}) custom-call(f32[512,1024]{1,0:T(8,128)} %table_hbm.1, f32[1,512]{1,0:T(1,128)} %bitcast.9, f32[448,512]{1,0:T(8,128)} %phase_hbm.1, s32[1,128]{1,0:T(1,128)} %bitcast.10, s32[1,128]{1,0:T(1,128)} %bitcast.11, s32[1,128]{1,0:T(1,128)} %bitcast.12, s32[1,128]{1,0:T(1,128)} %bitcast.13, ...), custom_call_target="tpu_custom_call" | custom-call | tf_op jit(solution)/shard_map/pallas_call | solution.py:583
  102.7 1.3 %copy.12 = f32[512,1024]{1,0:T(8,128)} copy(f32[512,1024]{1,0:T(8,128)S(1)} %get-tuple-element.8) | data formatting | bytes 4194304
  104.0 0.6 copy.13

commit v3 on v2

--- a/solution.py
+++ b/solution.py
@@ -245,25 +245,33 @@
 
     lax.fori_loop(0, tiles, fetch, 0)
 
-    def send_rows(buffer, source, target, sem):
+    def pack_rows(buffer, source, target):
         size = buffer.shape[0] // n_ent
+
+        def body(k, carry):
+            block = pl.ds(pl.multiple_of(k * size, 16), size)
+            source[block, :] = buffer[block, :].astype(BF16)
+            return carry
+
+        lax.fori_loop(0, n_ent, body, 0)
+        own = pl.ds(pl.multiple_of(ent * size, 16), size)
+        target[own, :] = buffer[own, :].astype(BF16)
+
+    def start_rows(source, target, sem):
+        size = target.shape[0] // n_ent
         own = pl.ds(pl.multiple_of(ent * size, 16), size)
         for k in range(1, n_ent):
             q = ent_peer(k)
             block = pl.ds(pl.multiple_of(q * size, 16), size)
-            source[block, :] = buffer[block, :].astype(BF16)
             remote(
                 source.at[block], target.at[own], sems.at[sem], sems.at[sem + 1], "ent", q
             ).start()
-        target[own, :] = buffer[own, :].astype(BF16)
-
-    def wait_rows(source, target, sem):
+
+    def all_rows(source, target, sem):
         most = pl.ds(0, target.shape[0] // n_ent * (n_ent - 1))
-        done = remote(
+        return remote(
             source.at[most], target.at[most], sems.at[sem], sems.at[sem + 1], "ent", ent_peer(1)
         )
-        done.wait_recv()
-        done.wait_send()
 
     def unpack(target, buffer):
         size = buffer.shape[0] // n_ent
@@ -284,7 +292,8 @@
             axis=1,
         ).astype(BF16)
 
-    send_rows(flat, rep_send, rep_recv, 2)
+    pack_rows(flat, rep_send, rep_recv)
+    start_rows(rep_send, rep_recv, 2)
 
     for load in loads[3:]:
         load.wait()
@@ -328,7 +337,9 @@
     lax.fori_loop(0, half // LANES, angles, 0)
     state_col[...] = to_column(state_ref[...])
 
-    wait_rows(rep_send, rep_recv, 2)
+    replies = all_rows(rep_send, rep_recv, 2)
+    replies.wait_recv()
+    replies.wait_send()
     unpack(rep_recv, flat)
 
     def rotate(j, sums):
@@ -384,7 +395,9 @@
             part = dot(pick_t[...], value)
             gr_flat[h][pl.ds(at, slots, stride=4), :] = part[:, :LANES]
             gr_flat[h][pl.ds(at + 1, slots, stride=4), :] = part[:, LANES:]
-        send_rows(gr_flat[h], gr_send.at[h], gr_recv.at[h], 4 + 2 * h)
+        pack_rows(gr_flat[h], gr_send.at[h], gr_recv.at[h])
+        if h == 0:
+            start_rows(gr_send.at[h], gr_recv.at[h], 4)
 
     scale = 2.0 / half
     turned = jnp.transpose(row_coef)
@@ -411,17 +424,15 @@
 
     theirs = pl.ds(pl.multiple_of((1 - core) * hrows, hrows), hrows)
     ours = pl.ds(pl.multiple_of(core * hrows, hrows), hrows)
-    longer, shorter = nz // 2, nz - 1 - nz // 2
 
     def rows_of(index):
         return pl.ds(pl.multiple_of(core * hrows + index * prow, prow), prow)
 
-    def ways(h):
-        lengths = (longer, shorter) if h == 0 else (shorter, longer)
-        return [(w, (1, -1)[w], lengths[w]) for w in range(2) if lengths[w] > 0]
-
     def chip(distance):
-        return lax.rem(z + distance + 2 * nz, nz)
+        return lax.rem(z + distance + nz, nz)
+
+    def part_of(w):
+        return pl.ds(w * quarter, quarter)
 
     def add_incoming(h, some):
         def body(part, carry):
@@ -448,7 +459,7 @@
         )
 
     def collect(h):
-        wait_rows(gr_send.at[h], gr_recv.at[h], 4 + 2 * h)
+        all_rows(gr_send.at[h], gr_recv.at[h], 4 + 2 * h).wait_recv()
         unpack(gr_recv.at[h], gr_flat[h])
         add_incoming(h, theirs)
         pair(h).start()
@@ -458,72 +469,111 @@
         pair(h).wait_recv()
         partial[h, ours, :] += pair_recv[h].astype(F32)
 
-    def ring(h, w, step, hop):
+    steps = (1, -1)
+
+    def ring(h, kind, w):
+        source, target = ring_send.at[h, kind, w], ring_recv.at[h, kind, w]
+        if kind == 0:
+            source, target = source.at[:, part_of(w)], target.at[:, part_of(w)]
         return remote(
-            ring_send.at[h, w, hop - 1],
-            ring_recv.at[h, w, hop - 1],
+            source,
+            target,
             sems.at[12 + h],
-            ring_sems.at[h, w, hop - 1],
+            ring_sems.at[h, kind, w],
             "dp",
-            2 * chip(step) + core,
+            2 * chip(steps[w] * (2, 1, 1, 2)[kind]) + core,
         )
 
-    def sum_hop(h, hop):
-        for w, step, length in ways(h):
-            if hop <= length:
-                value = partial[h, rows_of(chip(step * (length - hop + 1))), :]
-                if hop > 1:
-                    ring(h, w, step, hop - 1).wait_recv()
-                    value += ring_recv[h, w, hop - 2].astype(F32)
-                ring_send[h, w, hop - 1] = value.astype(BF16)
-                ring(h, w, step, hop).start()
+    def sum_first(h):
+        for kind in range(3):
+            for w in range(2):
+                piece = rows_of(chip(steps[w] * (4, 3, 1)[kind]))
+                columns = part_of(w) if kind == 0 else slice(None)
+                ring_send[h, kind, w, :, columns] = partial[h, piece, columns].astype(BF16)
+                ring(h, kind, w).start()
+
+    def sum_second(h):
+        for w in range(2):
+            ring(h, 1, w).wait_recv()
+            ring(h, 0, w).wait_recv()
+            value = partial[h, rows_of(chip(2 * steps[w])), :] + ring_recv[h, 1, w].astype(F32)
+            more = ring_recv[h, 0, w, :, part_of(w)].astype(F32)
+            same = slice(w * quarter, (w + 1) * quarter)
+            other = slice((1 - w) * quarter, (2 - w) * quarter)
+            ring_send[h, 3, w, :, part_of(w)] = (value[:, same] + more).astype(BF16)
+            ring_send[h, 3, w, :, part_of(1 - w)] = value[:, other].astype(BF16)
+            ring(h, 3, w).start()
 
     def sum_end(h):
         value = partial[h, rows_of(z), :]
-        for w, step, length in ways(h):
-            ring(h, w, step, length).wait_recv()
-            value += ring_recv[h, w, length - 1].astype(F32)
+        for kind in (2, 3):
+            for w in range(2):
+                ring(h, kind, w).wait_recv()
+                value += ring_recv[h, kind, w].astype(F32)
         total[h, rows_of(z), :] = value.astype(BF16)
 
-    def spread(h, w, step, hop):
-        piece = total.at[h, rows_of(chip(-step * (hop - 1)))]
+    def spread(h, kind, w):
+        begun = chip((0, 0, -2, -2)[kind] * steps[w])
+        piece = total.at[h, rows_of(begun)]
+        if kind == 3:
+            piece = piece.at[:, part_of(w)]
         return remote(
-            piece, piece, sems.at[14 + h], spread_sems.at[h, w, hop - 1], "dp", 2 * chip(step) + core
+            piece,
+            piece,
+            sems.at[14 + h],
+            spread_sems.at[h, kind, w],
+            "dp",
+            2 * chip(steps[w] * (2, 1, 1, 2)[kind]) + core,
         )
 
     def across(h, piece):
         return remote(piece, piece, sems.at[16 + 2 * h], sems.at[17 + 2 * h], "dp", partner)
 
-    def spread_hop(h, hop):
-        if hop == 1:
-            for w, step, length in ways(h):
-                spread(h, w, step, 1).start()
-            across(h, total.at[h, rows_of(z)]).start()
-            return
-        for w, step, length in ways(h):
-            if hop <= length + 1:
-                spread(h, w, step, hop - 1).wait_recv()
-                if hop <= length:
-                    spread(h, w, step, hop).start()
-                across(h, total.at[h, rows_of(chip(-step * (hop - 1)))]).start()
-
-    hops = longer
+    def cross(h, distance):
+        across(h, total.at[h, rows_of(chip(distance))]).start()
+
+    def spread_first(h):
+        for kind in (0, 1):
+            for w in range(2):
+                spread(h, kind, w).start()
+        cross(h, 0)
+
+    def spread_second(h):
+        for w in range(2):
+            spread(h, 0, w).wait_recv()
+            spread(h, 2, w).start()
+            spread(h, 3, w).start()
+            cross(h, -2 * steps[w])
+
+    def spread_end(h):
+        for kind, distance in ((1, 1), (2, 3)):
+            for w in range(2):
+                spread(h, kind, w).wait_recv()
+                cross(h, -distance * steps[w])
+        for w in range(2):
+            spread(h, 3, w).wait_recv()
+        cross(h, 4)
+
     own_part(0)
     own_part(1)
+    all_rows(gr_send.at[0], gr_recv.at[0], 4).wait_send()
+    start_rows(gr_send.at[1], gr_recv.at[1], 6)
     collect(0)
     take_pair(0)
-    for hop in range(1, hops + 1):
-        sum_hop(0, hop)
+    sum_first(0)
+    sum_second(0)
     sum_end(0)
-    spread_hop(0, 1)
+    spread_first(0)
     collect(1)
     take_pair(1)
-    for hop in range(1, hops + 1):
-        sum_hop(1, hop)
-        spread_hop(0, hop + 1)
+    sum_first(1)
+    spread_second(0)
+    sum_second(1)
+    spread_end(0)
     sum_end(1)
-    for hop in range(1, hops + 2):
-        spread_hop(1, hop)
+    spread_first(1)
+    spread_second(1)
+    spread_end(1)
 
     def update(first_row):
         def body(k, carry):
@@ -547,6 +597,7 @@
         across(h, total.at[h, theirs]).wait_recv()
     update((1 - core) * hrows)
     out_state[...] = to_row(state_col[...])
+    all_rows(gr_send.at[1], gr_recv.at[1], 6).wait_send()
     for h in range(2):
         pair(h).wait_send()
         pieces = pl.ds(0, (nz - 1) * prow)
@@ -619,16 +670,16 @@
             pltpu.VMEM((2, rows, half), F32),
             pltpu.VMEM((2, hrows, half), BF16),
             pltpu.VMEM((2, hrows, half), BF16),
-            pltpu.VMEM((2, 2, nz // 2, prow, half), BF16),
-            pltpu.VMEM((2, 2, nz // 2, prow, half), BF16),
+            pltpu.VMEM((2, 4, 2, prow, half), BF16),
+            pltpu.VMEM((2, 4, 2, prow, half), BF16),
             pltpu.VMEM((2, rows, half), BF16),
             pltpu.VMEM((rows, 1), F32),
             pltpu.VMEM((slots * chunks // 2, LANES), F32),
             pltpu.VMEM((slots * chunks // 2, LANES), F32),
             pltpu.SemaphoreType.DMA((20,)),
             pltpu.SemaphoreType.DMA((8,)),
-            pltpu.SemaphoreType.DMA((2, 2, nz // 2)),
-            pltpu.SemaphoreType.DMA((2, 2, nz // 2)),
+            pltpu.SemaphoreType.DMA((2, 4, 2)),
+            pltpu.SemaphoreType.DMA((2, 4, 2)),
         ],
         compiler_params=pltpu.CompilerParams(
             collective_id=0, has_side_effects=True, vmem_limit_bytes=48 * 1024 * 1024

time: 105 us -> 91.9 us (0.88)
  Pallas kernels: 102 us -> 88.7 us
    pallas_call x1, Pallas kernels: 102 us -> 88.7 us  [on_device(): pl.pallas_call(functools.partial(kernel, n_ent, n_dp, cap), out_shape=(ja...]
where the time goes in v3:
time: 91.9 us; the launch traced here: 91.2 us
  Pallas kernels  88.7 us (97%)
  local copies, waits for them, and re-layouts  1.9 us (2%)
    pallas_call x1, Pallas kernels, on_device(): pl.pallas_call(functools.partial(kernel, n_ent, n_dp, cap), out_shape=(ja...  88.7 us
    unnamed x2, local copies, waits for them, and re-layouts  1.9 us

profile of v3, /device:TPU:1, one launch (start us, length us, event | category | flops | bytes accessed | tf_op | source)
XLA Modules:
  0.0 91.2 jit_solution(8700906103307581283)
XLA Ops:
  0.6 88.7 %shard_map.95 = (f32[512,1024]{1,0:T(8,128)S(1)}, f32[1,512]{1,0:T(1,128)S(1)}) custom-call(f32[512,1024]{1,0:T(8,128)} %table_hbm.1, f32[1,512]{1,0:T(1,128)} %bitcast.9, f32[448,512]{1,0:T(8,128)} %phase_hbm.1, s32[1,128]{1,0:T(1,128)} %bitcast.10, s32[1,128]{1,0:T(1,128)} %bitcast.11, s32[1,128]{1,0:T(1,128)} %bitcast.12, s32[1,128]{1,0:T(1,128)} %bitcast.13, ...), custom_call_target="tpu_custom_call" | custom-call | tf_op jit(solution)/shard_map/pallas_call | solution.py:634
  89.3 1.3 %copy.12 = f32[512,1024]{1,0:T(8,128)} copy(f32[512,1024]{1,0:T(8,128)S(1)} %get-tuple-element.8) | data formatting | bytes 4194304
  90.6 0.6 copy.13

commit v4 on v3

--- a/solution.py
+++ b/solution.py
@@ -104,6 +104,7 @@
     load_sems,
     ring_sems,
     spread_sems,
+    across_sems,
 ):
     rows, width = table.shape
     half = width // 2
@@ -526,11 +527,17 @@
             2 * chip(steps[w] * (2, 1, 1, 2)[kind]) + core,
         )
 
-    def across(h, piece):
-        return remote(piece, piece, sems.at[16 + 2 * h], sems.at[17 + 2 * h], "dp", partner)
+    def across(h, distance, side):
+        half_rows = (core + side - 2 * core * side) * hrows
+        piece = total.at[
+            h, pl.ds(pl.multiple_of(half_rows + chip(distance) * prow, prow), prow)
+        ]
+        return remote(
+            piece, piece, sems.at[16 + h], across_sems.at[h, distance + 3], "dp", partner
+        )
 
     def cross(h, distance):
-        across(h, total.at[h, rows_of(chip(distance))]).start()
+        across(h, distance, 0).start()
 
     def spread_first(h):
         for kind in (0, 1):
@@ -545,14 +552,35 @@
             spread(h, 3, w).start()
             cross(h, -2 * steps[w])
 
-    def spread_end(h):
-        for kind, distance in ((1, 1), (2, 3)):
-            for w in range(2):
-                spread(h, kind, w).wait_recv()
-                cross(h, -distance * steps[w])
+    def spread_near(h):
+        for w in range(2):
+            spread(h, 1, w).wait_recv()
+            cross(h, -steps[w])
+
+    def spread_far(h):
+        for w in range(2):
+            spread(h, 2, w).wait_recv()
+            cross(h, -3 * steps[w])
         for w in range(2):
             spread(h, 3, w).wait_recv()
         cross(h, 4)
+
+    def update(distance, side):
+        if side == 1:
+            for h in range(2):
+                across(h, distance, 1).wait_recv()
+        half_rows = (core + side - 2 * core * side) * hrows
+        block = pl.ds(pl.multiple_of(half_rows + chip(distance) * prow, prow), prow)
+        values = [total[h, block, :].astype(F32) for h in range(2)]
+        square = values[0] * values[0] + values[1] * values[1]
+        new = state_col[block, :] + jnp.sum(square, axis=1, keepdims=True) / width
+        state_col[block, :] = new
+        rate = LEARN_RATE / jnp.sqrt(new)
+        for h in range(2):
+            for part in range(2):
+                columns = pl.ds(part * half + h * quarter, quarter)
+                value = values[h][:, part * quarter : (part + 1) * quarter]
+                out_table[block, columns] = table[block, columns] - value * rate
 
     own_part(0)
     own_part(1)
@@ -562,49 +590,35 @@
     take_pair(0)
     sum_first(0)
     sum_second(0)
+    collect(1)
     sum_end(0)
     spread_first(0)
-    collect(1)
     take_pair(1)
     sum_first(1)
     spread_second(0)
     sum_second(1)
-    spread_end(0)
+    spread_near(0)
     sum_end(1)
     spread_first(1)
+    spread_far(0)
     spread_second(1)
-    spread_end(1)
-
-    def update(first_row):
-        def body(k, carry):
-            block = pl.ds(pl.multiple_of(first_row + k * 32, 32), 32)
-            values = [total[h, block, :].astype(F32) for h in range(2)]
-            square = values[0] * values[0] + values[1] * values[1]
-            new = state_col[block, :] + jnp.sum(square, axis=1, keepdims=True) / width
-            state_col[block, :] = new
-            rate = LEARN_RATE / jnp.sqrt(new)
-            for h in range(2):
-                for part in range(2):
-                    columns = pl.ds(part * half + h * quarter, quarter)
-                    value = values[h][:, part * quarter : (part + 1) * quarter]
-                    out_table[block, columns] = table[block, columns] - value * rate
-            return carry
-
-        lax.fori_loop(0, hrows // 32, body, 0)
-
-    update(core * hrows)
-    for h in range(2):
-        across(h, total.at[h, theirs]).wait_recv()
-    update((1 - core) * hrows)
+    spread_near(1)
+    for side in range(2):
+        for distance in (0, 2, -2, 1, -1):
+            update(distance, side)
+    spread_far(1)
+    for side in range(2):
+        for distance in (3, -3, 4):
+            update(distance, side)
     out_state[...] = to_row(state_col[...])
     all_rows(gr_send.at[1], gr_recv.at[1], 6).wait_send()
     for h in range(2):
         pair(h).wait_send()
-        pieces = pl.ds(0, (nz - 1) * prow)
-        piece = total.at[h, pieces]
-        remote(piece, piece, sems.at[12 + h], sems.at[12 + h], "dp", partner).wait_send()
-        remote(piece, piece, sems.at[14 + h], sems.at[14 + h], "dp", partner).wait_send()
-        across(h, total.at[h, ours]).wait_send()
+        pieces = total.at[h, pl.ds(0, (nz - 1) * prow)]
+        remote(pieces, pieces, sems.at[12 + h], sems.at[12 + h], "dp", partner).wait_send()
+        remote(pieces, pieces, sems.at[14 + h], sems.at[14 + h], "dp", partner).wait_send()
+        pieces = total.at[h, ours]
+        remote(pieces, pieces, sems.at[16 + h], sems.at[16 + h], "dp", partner).wait_send()
 
 
 def on_device(
@@ -680,6 +694,7 @@
             pltpu.SemaphoreType.DMA((8,)),
             pltpu.SemaphoreType.DMA((2, 4, 2)),
             pltpu.SemaphoreType.DMA((2, 4, 2)),
+            pltpu.SemaphoreType.DMA((2, 8)),
         ],
         compiler_params=pltpu.CompilerParams(
             collective_id=0, has_side_effects=True, vmem_limit_bytes=48 * 1024 * 1024

time: 91.9 us -> 90.3 us (0.983)
  Pallas kernels: 88.7 us -> 87.6 us
    pallas_call x1, Pallas kernels: 88.7 us -> 87.6 us  [on_device(): pl.pallas_call(functools.partial(kernel, n_ent, n_dp, cap), out_shape=(ja...]
where the time goes in v4:
time: 90.3 us; the launch traced here: 90.1 us
  Pallas kernels  87.6 us (97%)
  local copies, waits for them, and re-layouts  1.9 us (2%)
    pallas_call x1, Pallas kernels, on_device(): pl.pallas_call(functools.partial(kernel, n_ent, n_dp, cap), out_shape=(ja...  87.6 us
    unnamed x2, local copies, waits for them, and re-layouts  1.9 us

profile of v4, /device:TPU:1, one launch (start us, length us, event | category | flops | bytes accessed | tf_op | source)
XLA Modules:
  0.0 90.1 jit_solution(3999568852404274769)
XLA Ops:
  0.6 87.6 %shard_map.95 = (f32[512,1024]{1,0:T(8,128)S(1)}, f32[1,512]{1,0:T(1,128)S(1)}) custom-call(f32[512,1024]{1,0:T(8,128)} %table_hbm.1, f32[1,512]{1,0:T(1,128)} %bitcast.9, f32[448,512]{1,0:T(8,128)} %phase_hbm.1, s32[1,128]{1,0:T(1,128)} %bitcast.10, s32[1,128]{1,0:T(1,128)} %bitcast.11, s32[1,128]{1,0:T(1,128)} %bitcast.12, s32[1,128]{1,0:T(1,128)} %bitcast.13, ...), custom_call_target="tpu_custom_call" | custom-call | tf_op jit(solution)/shard_map/pallas_call | solution.py:648
  88.2 1.3 %copy.12 = f32[512,1024]{1,0:T(8,128)} copy(f32[512,1024]{1,0:T(8,128)S(1)} %get-tuple-element.8) | data formatting | bytes 4194304
  89.5 0.6 copy.13

commit v5 on v4

--- a/solution.py
+++ b/solution.py
@@ -73,7 +73,6 @@
     rel_ref,
     tail_ref,
     neg_ref,
-    flat,
     req_send,
     req_recv,
     rep_send,
@@ -134,6 +133,12 @@
     def shift(m, n):
         return ((m + 1) // 2 if m % 2 else -(m // 2)) % n
 
+    def hops(k):
+        dy, dx = shift(k % ny, ny), k // ny
+        return min(dy, ny - dy) + min(dx, nx - dx)
+
+    far_first = sorted(range(1, n_ent), key=hops, reverse=True)
+
     def ent_peer(k):
         return lax.rem(y + shift(k % ny, ny), ny) * nx + lax.rem(x + k // ny, nx)
 
@@ -175,7 +180,7 @@
             barrier, inc=1, device_id={axis: index}, device_id_type=pl.DeviceIdType.MESH
         )
 
-    for k in range(1, n_ent):
+    for k in far_first:
         greet("ent", ent_peer(k))
     for k in range(1, nz):
         greet("dp", 2 * z_peer(k) + core)
@@ -203,7 +208,7 @@
 
     pl.semaphore_wait(barrier, n_ent - 1 + nz - 1 + 1)
 
-    for k in range(1, n_ent):
+    for k in far_first:
         q = ent_peer(k)
         remote(req_send.at[q], req_recv.at[ent], sems.at[0], sems.at[1], "ent", q).start()
     req_recv[ent] = req_send[ent]
@@ -237,14 +242,12 @@
     ask_col = to_column(ask_row)
     asked_t[...] = onehot(ask_col == iota((slots, rows), 1))
 
-    def fetch(j, carry):
-        columns = pl.ds(pl.multiple_of(j * tile, tile), tile)
-        part = dot(asked_t[...], table_bf[:, columns])
-        flat[pl.ds(2 * j, slots, stride=chunks), :] = part[:, :LANES]
-        flat[pl.ds(2 * j + 1, slots, stride=chunks), :] = part[:, LANES:]
-        return carry
-
-    lax.fori_loop(0, tiles, fetch, 0)
+    def fetch(h):
+        for part in range(2):
+            columns = pl.ds(part * half + h * tile, tile)
+            value = dot(asked_t[...], table_bf[:, columns])
+            gr_flat[h][pl.ds(2 * part, slots, stride=4), :] = value[:, :LANES]
+            gr_flat[h][pl.ds(2 * part + 1, slots, stride=4), :] = value[:, LANES:]
 
     def pack_rows(buffer, source, target):
         size = buffer.shape[0] // n_ent
@@ -261,7 +264,7 @@
     def start_rows(source, target, sem):
         size = target.shape[0] // n_ent
         own = pl.ds(pl.multiple_of(ent * size, 16), size)
-        for k in range(1, n_ent):
+        for k in far_first:
             q = ent_peer(k)
             block = pl.ds(pl.multiple_of(q * size, 16), size)
             remote(
@@ -284,17 +287,20 @@
 
         lax.fori_loop(0, n_ent, body, 0)
 
-    def slot_tile(j):
+    def slot_tile(h, part):
         return jnp.concatenate(
             [
-                flat[pl.ds(2 * j, slots, stride=chunks), :],
-                flat[pl.ds(2 * j + 1, slots, stride=chunks), :],
+                gr_flat[h][pl.ds(2 * part, slots, stride=4), :],
+                gr_flat[h][pl.ds(2 * part + 1, slots, stride=4), :],
             ],
             axis=1,
         ).astype(BF16)
 
-    pack_rows(flat, rep_send, rep_recv)
-    start_rows(rep_send, rep_recv, 2)
+    for h in range(2):
+        fetch(h)
+        pack_rows(gr_flat[h], rep_send.at[h], rep_recv.at[h])
+        if h == 0:
+            start_rows(rep_send.at[h], rep_recv.at[h], 2)
 
     for load in loads[3:]:
         load.wait()
@@ -325,6 +331,8 @@
 
     row_sq[...] = to_row(lax.fori_loop(0, tiles, tails, jnp.zeros((rows, 1), F32)))
 
+    all_rows(rep_send.at[0], rep_recv.at[0], 2).wait_send()
+    start_rows(rep_send.at[1], rep_recv.at[1], 18)
     rel_pick = onehot(to_column(rel_ref[...]) == iota((tri, rels), 1))
 
     def angles(j, carry):
@@ -338,17 +346,16 @@
     lax.fori_loop(0, half // LANES, angles, 0)
     state_col[...] = to_column(state_ref[...])
 
-    replies = all_rows(rep_send, rep_recv, 2)
-    replies.wait_recv()
-    replies.wait_send()
-    unpack(rep_recv, flat)
-
-    def rotate(j, sums):
-        sums_rot, sums_diff = sums
-        re = pl.ds(pl.multiple_of(j * tile, tile), tile)
-        im = pl.ds(pl.multiple_of(half + j * tile, tile), tile)
-        head_re = dot(pick[...], slot_tile(j))
-        head_im = dot(pick[...], slot_tile(j + tiles // 2))
+    rot_sq = jnp.zeros((tri, 1), F32)
+    diff_sq = jnp.zeros((tri, 1), F32)
+    scores = jnp.zeros((tri, rows), F32)
+    for h in range(2):
+        all_rows(rep_send.at[h], rep_recv.at[h], (2, 18)[h]).wait_recv()
+        unpack(rep_recv.at[h], gr_flat[h])
+        re = pl.ds(h * tile, tile)
+        im = pl.ds(half + h * tile, tile)
+        head_re = dot(pick[...], slot_tile(h, 0))
+        head_im = dot(pick[...], slot_tile(h, 1))
         cos, sin = cosine[:, re], sine[:, re]
         rot_re = head_re * cos - head_im * sin
         rot_im = head_re * sin + head_im * cos
@@ -356,14 +363,11 @@
         rotated[:, im] = rot_im
         diff_re = rot_re - positive[:, re]
         diff_im = rot_im - positive[:, im]
-        sums_rot += jnp.sum(rot_re * rot_re + rot_im * rot_im, axis=1, keepdims=True)
-        sums_diff += jnp.sum(diff_re * diff_re + diff_im * diff_im, axis=1, keepdims=True)
-        return sums_rot, sums_diff
-
-    nothing = jnp.zeros((tri, 1), F32)
-    rot_sq, diff_sq = lax.fori_loop(0, tiles // 2, rotate, (nothing, nothing))
-    rotated_bf = rotated[...].astype(BF16)
-    scores = dot_nt(rotated_bf, table_bf[...])
+        rot_sq += jnp.sum(rot_re * rot_re + rot_im * rot_im, axis=1, keepdims=True)
+        diff_sq += jnp.sum(diff_re * diff_re + diff_im * diff_im, axis=1, keepdims=True)
+        scores += dot_nt(rot_re.astype(BF16), table_bf[:, re])
+        scores += dot_nt(rot_im.astype(BF16), table_bf[:, im])
+    all_rows(rep_send.at[1], rep_recv.at[1], 18).wait_send()
     distance = (rot_sq + row_sq[...] - 2.0 * scores) * (1.0 / half)
     dist_pos = diff_sq * (1.0 / half)
     logits = MARGIN - distance
@@ -436,23 +440,14 @@
         return pl.ds(w * quarter, quarter)
 
     def add_incoming(h, some):
-        def body(part, carry):
-            columns = pl.ds(pl.multiple_of(part * quarter, quarter), quarter)
-            value = jnp.concatenate(
-                [
-                    gr_flat[h][pl.ds(2 * part, slots, stride=4), :],
-                    gr_flat[h][pl.ds(2 * part + 1, slots, stride=4), :],
-                ],
-                axis=1,
-            ).astype(BF16)
+        for part in range(2):
+            columns = pl.ds(part * quarter, quarter)
+            value = slot_tile(h, part)
             sums = partial[h, some, columns] + dot(asked[some, :], value)
             if some is theirs:
                 pair_send[h, :, columns] = sums.astype(BF16)
             else:
                 partial[h, some, columns] = sums
-            return carry
-
-        lax.fori_loop(0, 2, body, 0)
 
     def pair(h):
         return remote(
@@ -663,11 +658,10 @@
             pltpu.VMEM((1, tri), jnp.int32),
             pltpu.VMEM((1, tri), jnp.int32),
             pltpu.VMEM((1, negs), jnp.int32),
-            pltpu.VMEM((slots * chunks, LANES), F32),
             pltpu.VMEM((n_ent, 1, LANES), F32),
             pltpu.VMEM((n_ent, 1, LANES), F32),
-            pltpu.VMEM((slots * chunks, LANES), BF16),
-            pltpu.VMEM((slots * chunks, LANES), BF16),
+            pltpu.VMEM((2, slots * chunks // 2, LANES), BF16),
+            pltpu.VMEM((2, slots * chunks // 2, LANES), BF16),
             pltpu.VMEM((2, slots * chunks // 2, LANES), BF16),
             pltpu.VMEM((2, slots * chunks // 2, LANES), BF16),
             pltpu.VMEM((tri, slots), BF16),

time: 90.3 us -> 87.9 us (0.973)
  Pallas kernels: 87.6 us -> 85.3 us
    pallas_call x1, Pallas kernels: 87.6 us -> 85.3 us  [on_device(): pl.pallas_call(functools.partial(kernel, n_ent, n_dp, cap), out_shape=(ja...]
where the time goes in v5:
time: 87.9 us; the launch traced here: 87.8 us
  Pallas kernels  85.3 us (97%)
  local copies, waits for them, and re-layouts  1.9 us (2%)
    pallas_call x1, Pallas kernels, on_device(): pl.pallas_call(functools.partial(kernel, n_ent, n_dp, cap), out_shape=(ja...  85.3 us
    unnamed x2, local copies, waits for them, and re-layouts  1.9 us

profile of v5, /device:TPU:1, one launch (start us, length us, event | category | flops | bytes accessed | tf_op | source)
XLA Modules:
  0.0 87.8 jit_solution(18122083202131482411)
XLA Ops:
  0.6 85.3 %shard_map.95 = (f32[512,1024]{1,0:T(8,128)S(1)}, f32[1,512]{1,0:T(1,128)S(1)}) custom-call(f32[512,1024]{1,0:T(8,128)} %table_hbm.1, f32[1,512]{1,0:T(1,128)} %bitcast.9, f32[448,512]{1,0:T(8,128)} %phase_hbm.1, s32[1,128]{1,0:T(1,128)} %bitcast.10, s32[1,128]{1,0:T(1,128)} %bitcast.11, s32[1,128]{1,0:T(1,128)} %bitcast.12, s32[1,128]{1,0:T(1,128)} %bitcast.13, ...), custom_call_target="tpu_custom_call" | custom-call | tf_op jit(solution)/shard_map/pallas_call | solution.py:643
  85.9 1.3 %copy.12 = f32[512,1024]{1,0:T(8,128)} copy(f32[512,1024]{1,0:T(8,128)S(1)} %get-tuple-element.8) | data formatting | bytes 4194304
  87.2 0.6 copy.13

commit v6 on v5

--- a/solution.py
+++ b/solution.py
@@ -170,8 +170,6 @@
             )
         )
     ]
-    for load in loads:
-        load.start()
 
     barrier = pltpu.get_barrier_semaphore()
 
@@ -185,6 +183,8 @@
     for k in range(1, nz):
         greet("dp", 2 * z_peer(k) + core)
     greet("dp", partner)
+    for load in loads:
+        load.start()
 
     loads[0].wait()
     loads[1].wait()

time: 87.9 us -> 87.9 us (level)
  no operation moved by 1% of the time
where the time goes in v6:
time: 87.9 us; the launch traced here: 87.8 us
  Pallas kernels  85.2 us (97%)
  local copies, waits for them, and re-layouts  1.9 us (2%)
    pallas_call x1, Pallas kernels, on_device(): pl.pallas_call(functools.partial(kernel, n_ent, n_dp, cap), out_shape=(ja...  85.2 us
    unnamed x2, local copies, waits for them, and re-layouts  1.9 us

profile of v6, /device:TPU:1, one launch (start us, length us, event | category | flops | bytes accessed | tf_op | source)
XLA Modules:
  0.0 87.8 jit_solution(17343686425936207356)
XLA Ops:
  0.6 85.2 %shard_map.95 = (f32[512,1024]{1,0:T(8,128)S(1)}, f32[1,512]{1,0:T(1,128)S(1)}) custom-call(f32[512,1024]{1,0:T(8,128)} %table_hbm.1, f32[1,512]{1,0:T(1,128)} %bitcast.9, f32[448,512]{1,0:T(8,128)} %phase_hbm.1, s32[1,128]{1,0:T(1,128)} %bitcast.10, s32[1,128]{1,0:T(1,128)} %bitcast.11, s32[1,128]{1,0:T(1,128)} %bitcast.12, s32[1,128]{1,0:T(1,128)} %bitcast.13, ...), custom_call_target="tpu_custom_call" | custom-call | tf_op jit(solution)/shard_map/pallas_call | solution.py:643
  85.9 1.3 %copy.12 = f32[512,1024]{1,0:T(8,128)} copy(f32[512,1024]{1,0:T(8,128)S(1)} %get-tuple-element.8) | data formatting | bytes 4194304
  87.2 0.6 copy.13
